TPU v7x, 512 devices: a whole 4x4x16 slice. The times are simulated.
512 devices in a mesh: batch: 32 (over y, x, core), seq: 16 (over z).
Axes of the slice: x: 4, y: 4, z: 16, core: 2. Of those that a mesh axis runs over, the one named last changes fastest.
Arguments:
- events: bfloat16 [131072, 256], P(('batch', 'seq')), parts along dimension 0, may hold values from -6 to 6
- positions: int32 [131072], P(('batch', 'seq')), parts along dimension 0, may hold values from 0 to 4095, as said below
- length: int32 [32], P('batch'), parts along dimension 0, may hold values from 2048 to 4096
- filters: float32 [4096, 2, 256], P('seq'), may hold values from -0.09375 to 0.09375
- skip_gain: float32 [2, 256], replicated, may hold values from 0.5 to 1.5
- short_filter: float32 [3, 768], replicated, may hold values from -3 to 3
- in_proj: bfloat16 [256, 768], replicated, may hold values from -0.375 to 0.375
- out_proj: bfloat16 [256, 256], replicated, may hold values from -0.375 to 0.375
Outputs:
- layer_out: bfloat16 [131072, 256], P(('batch', 'seq')), parts along dimension 0
There are 32 independent parts, one for each index of `batch`. A program takes and returns all parts, laid end to end along the dimension named above; an argument that names none is the same for every part. Nothing has to cross between parts.
Inputs may be any that keep to these rules, and one draw needn't show every extreme that they name: positions is a permutation of 0 to 4095. Cut each row block b (positions b * 256 to (b + 1) * 256 - 1) into runs of 16 positions, run c starting at b * 256 + c * 16. The rows of one seq device hold whole runs only, exactly one run of each row block and exactly one run of each index c, in any order.
All inputs are finite; a program needn't handle non-finite values.
Results may differ from a plain program's by a relative error of at most 0.007.
Values may be sent and summed in bfloat16 or wider, within the bound.
A program may use at most 64 MiB of HBM per device.

v0:
```python
import math

import jax
import jax.numpy as jnp
from jax import lax
from jax.sharding import PartitionSpec as P


def passed_along(value, axis, steps):
    count = lax.axis_size(axis)
    first, last = (max(0, -steps), min(count, count - steps))
    return lax.ppermute(value, axis, [(source, source + steps) for source in range(first, last)])


def product(form, left, right):
    return jnp.einsum(form, left, right, precision=lax.Precision.HIGHEST)


def make_tables(dev_count, col_size, tok_rows, device):
    points = 2 * dev_count * tok_rows
    freq_outer = jnp.arange(2 * dev_count, dtype=jnp.int32)
    time_outer = jnp.arange(dev_count, dtype=jnp.int32)
    outer_angle = (freq_outer[:, None] * time_outer[None, :] % (2 * dev_count)).astype(
        jnp.float32
    ) * (2.0 * math.pi / (2 * dev_count))
    time_inner = device * col_size + jnp.arange(col_size, dtype=jnp.int32)
    twist_angle = (freq_outer[:, None] * time_inner[None, :] % points).astype(jnp.float32) * (
        2.0 * math.pi / points
    )
    index_inner = jnp.arange(tok_rows, dtype=jnp.int32)
    inner_angle = (index_inner[:, None] * index_inner[None, :] % tok_rows).astype(jnp.float32) * (
        2.0 * math.pi / tok_rows
    )
    return (
        jnp.cos(outer_angle),
        jnp.sin(outer_angle),
        jnp.cos(twist_angle)[:, :, None],
        jnp.sin(twist_angle)[:, :, None],
        jnp.cos(inner_angle),
        jnp.sin(inner_angle),
        float(points),
    )


def forward(columns, tables):
    cos_outer, sin_outer, cos_twist, sin_twist, cos_inner, sin_inner, points = tables
    real_part = product("kn,nqc->kqc", cos_outer, columns)
    imag_part = -product("kn,nqc->kqc", sin_outer, columns)
    twist_real = real_part * cos_twist + imag_part * sin_twist
    twist_imag = imag_part * cos_twist - real_part * sin_twist
    freq_real, freq_imag = (
        lax.all_to_all(twist_real, "seq", split_axis=0, concat_axis=1, tiled=True),
        lax.all_to_all(twist_imag, "seq", split_axis=0, concat_axis=1, tiled=True),
    )
    out_real = product("kn,jnc->jkc", cos_inner, freq_real) + product(
        "kn,jnc->jkc", sin_inner, freq_imag
    )
    out_imag = product("kn,jnc->jkc", cos_inner, freq_imag) - product(
        "kn,jnc->jkc", sin_inner, freq_real
    )
    return (out_real, out_imag)


def inverse(spec_real, spec_imag, tables):
    cos_outer, sin_outer, cos_twist, sin_twist, cos_inner, sin_inner, points = tables
    back_real = product("nk,jkc->jnc", cos_inner, spec_real) - product(
        "nk,jkc->jnc", sin_inner, spec_imag
    )
    back_imag = product("nk,jkc->jnc", cos_inner, spec_imag) + product(
        "nk,jkc->jnc", sin_inner, spec_real
    )
    cols_real, cols_imag = (
        lax.all_to_all(back_real, "seq", split_axis=1, concat_axis=0, tiled=True),
        lax.all_to_all(back_imag, "seq", split_axis=1, concat_axis=0, tiled=True),
    )
    turn_real = cols_real * cos_twist - cols_imag * sin_twist
    turn_imag = cols_imag * cos_twist + cols_real * sin_twist
    summed = product("kn,kqc->nqc", cos_outer, turn_real) - product(
        "kn,kqc->nqc", sin_outer, turn_imag
    )
    return summed / points


def body(events, positions, length, filters, skip_gain, short_filter, in_proj, out_proj):
    tok_rows, features = events.shape
    dev_count = lax.axis_size("seq")
    col_size = tok_rows // dev_count
    device = lax.axis_index("seq")
    local_ids = jnp.arange(tok_rows, dtype=jnp.int32)
    owners = positions // tok_rows
    slot_ids = positions % tok_rows
    global_pos = device * tok_rows + local_ids
    sort_order = jnp.argsort(owners, stable=True)
    sent_rows = events[sort_order].reshape(dev_count, col_size, features)
    sent_slots = slot_ids[sort_order].reshape(dev_count, col_size)
    received, recv_slots = (
        lax.all_to_all(sent_rows, "seq", split_axis=0, concat_axis=0, tiled=True),
        lax.all_to_all(sent_slots, "seq", split_axis=0, concat_axis=0, tiled=True),
    )
    placing = jnp.argsort(recv_slots.reshape(-1))
    stream = received.reshape(tok_rows, features)[placing]
    stream = jnp.where((global_pos < length[0])[:, None], stream, jnp.zeros_like(stream))
    projected = jnp.dot(stream, in_proj, preferred_element_type=jnp.float32).astype(jnp.bfloat16)
    tables = make_tables(dev_count, col_size, tok_rows, device)
    before = passed_along(projected[tok_rows - 2 :], "seq", 1)
    extended = jnp.concatenate([before, projected], axis=0).astype(jnp.float32)
    shorted = (
        short_filter[0] * extended[2:]
        + short_filter[1] * extended[1:-1]
        + short_filter[2] * extended[:-2]
    )
    value = shorted[:, :features]
    gate_one = shorted[:, features : 2 * features]
    gate_two = shorted[:, 2 * features :]
    filter_cols = lax.all_to_all(
        filters.reshape(dev_count, col_size, 2 * features),
        "seq",
        split_axis=0,
        concat_axis=0,
        tiled=True,
    )
    filt_real, filt_imag = forward(filter_cols, tables)

    def convolve(signal, which):
        taps_real = filt_real[:, :, which * features : (which + 1) * features]
        taps_imag = filt_imag[:, :, which * features : (which + 1) * features]
        columns = lax.all_to_all(
            signal.reshape(dev_count, col_size, features),
            "seq",
            split_axis=0,
            concat_axis=0,
            tiled=True,
        )
        sig_real, sig_imag = forward(columns, tables)
        prod_real = sig_real * taps_real - sig_imag * taps_imag
        prod_imag = sig_real * taps_imag + sig_imag * taps_real
        result = inverse(prod_real, prod_imag, tables)
        return lax.all_to_all(result, "seq", split_axis=0, concat_axis=0, tiled=True).reshape(
            tok_rows, features
        )

    first = gate_one * (convolve(value, 0) + skip_gain[0] * value)
    second = convolve(first, 1) + skip_gain[1] * first
    gated = (gate_two * second).astype(jnp.bfloat16)
    layer_out = jnp.dot(gated, out_proj, preferred_element_type=jnp.float32).astype(jnp.bfloat16)
    return layer_out


def solution(mesh):
    return jax.shard_map(
        body,
        mesh=mesh,
        in_specs=(
            P(("batch", "seq"), None),
            P(("batch", "seq")),
            P("batch"),
            P("seq", None, None),
            P(),
            P(),
            P(),
            P(),
        ),
        out_specs=P(("batch", "seq"), None),
        check_vma=False,
    )
```

profile of v0, /device:TPU:6, one launch (start us, length us, event | category | flops | bytes accessed | tf_op | source)
XLA Modules:
  0.0 622.9 jit_solution(13456327397430032435)
XLA Ops:
  6.6 15.2 %all-to-all-start.1 = ((s32[16,1,16]{2,1,0:T(1,128)}), s32[16,1,16]{2,1,0:T(1,128)S(1)}, u32[]{:S(2)}, u32[]{:S(2)}) async-start(s32[16,1,16]{2,1,0:T(1,128)} %all_to_all.155), calls=%async_computation.1 | async-start | bytes 16384 | tf_op jit(solution)/shard_map/all_to_all | solution.py:98
  23.6 10.6 %all-to-all-done.1 = s32[16,1,16]{2,1,0:T(1,128)S(1)} async-done(((s32[16,1,16]{2,1,0:T(1,128)}), s32[16,1,16]{2,1,0:T(1,128)S(1)}, u32[]{:S(2)}, u32[]{:S(2)}) %all-to-all-start.1) | async-done | bytes 1056 | tf_op jit(solution)/shard_map/all_to_all | solution.py:98
  42.9 8.6 %all-to-all-done = bf16[16,16,256]{2,1,0:T(8,128)(2,1)S(1)} async-done(((bf16[16,16,256]{2,1,0:T(8,128)(2,1)}), bf16[16,16,256]{2,1,0:T(8,128)(2,1)S(1)}, u32[]{:S(2)}, u32[]{:S(2)}) %all-to-all-start) | async-done | bytes 131104 | tf_op jit(solution)/shard_map/all_to_all | solution.py:97
  58.1 6.2 all-to-all-start.2
  65.6 15.3 %all-to-all-done.2 = f32[16,16,256]{2,1,0:T(8,128)S(1)} async-done(((f32[16,16,256]{2,1,0:T(8,128)}), f32[16,16,256]{2,1,0:T(8,128)S(1)}, u32[]{:S(2)}, u32[]{:S(2)}) %all-to-all-start.2) | async-done | bytes 262176 | tf_op jit(solution)/shard_map/all_to_all | solution.py:127
  80.8 5.1 all-to-all-start.5
  88.8 22.7 %all-to-all-done.5 = f32[16,16,512]{2,1,0:T(8,128)S(1)} async-done(((f32[16,16,512]{2,1,0:T(8,128)}), f32[16,16,512]{2,1,0:T(8,128)S(1)}, u32[]{:S(2)}, u32[]{:S(2)}) %all-to-all-start.5) | async-done | bytes 524320 | tf_op jit(solution)/shard_map/all_to_all | solution.py:115
  111.4 7.5 %all-to-all-start.3 = ((f32[32,16,256]{2,1,0:T(8,128)}), f32[32,16,256]{2,1,0:T(8,128)S(1)}, u32[]{:S(2)}, u32[]{:S(2)}) async-start(f32[32,16,256]{2,1,0:T(8,128)} %copy.94), calls=%async_computation.3 | async-start | bytes 1048576 | tf_op jit(solution)/shard_map/all_to_all | solution.py:52
  120.1 25.9 %all-to-all-done.3 = f32[32,16,256]{2,1,0:T(8,128)S(1)} async-done(((f32[32,16,256]{2,1,0:T(8,128)}), f32[32,16,256]{2,1,0:T(8,128)S(1)}, u32[]{:S(2)}, u32[]{:S(2)}) %all-to-all-start.3) | async-done | bytes 524320 | tf_op jit(solution)/shard_map/all_to_all | solution.py:52
  146.0 7.1 %all-to-all-start.4 = ((f32[32,16,256]{2,1,0:T(8,128)}), f32[32,16,256]{2,1,0:T(8,128)}, u32[]{:S(2)}, u32[]{:S(2)}) async-start(f32[32,16,256]{2,1,0:T(8,128)} %copy.97), calls=%async_computation.4 | async-start | bytes 1048576 | tf_op jit(solution)/shard_map/all_to_all | solution.py:53
  157.4 24.2 %all-to-all-done.4 = f32[32,16,256]{2,1,0:T(8,128)} async-done(((f32[32,16,256]{2,1,0:T(8,128)}), f32[32,16,256]{2,1,0:T(8,128)}, u32[]{:S(2)}, u32[]{:S(2)}) %all-to-all-start.4) | async-done | bytes 524320 | tf_op jit(solution)/shard_map/all_to_all | solution.py:53
  181.6 6.6 %all-to-all-start.7 = ((f32[32,16,512]{2,1,0:T(8,128)}), f32[32,16,512]{2,1,0:T(8,128)S(1)}, u32[]{:S(2)}, u32[]{:S(2)}) async-start(f32[32,16,512]{2,1,0:T(8,128)} %copy.105), calls=%async_computation.7 | async-start | bytes 2097152 | tf_op jit(solution)/shard_map/all_to_all | solution.py:53
  189.7 47.9 %all-to-all-done.7 = f32[32,16,512]{2,1,0:T(8,128)S(1)} async-done(((f32[32,16,512]{2,1,0:T(8,128)}), f32[32,16,512]{2,1,0:T(8,128)S(1)}, u32[]{:S(2)}, u32[]{:S(2)}) %all-to-all-start.7) | async-done | bytes 1048608 | tf_op jit(solution)/shard_map/all_to_all | solution.py:53
  238.6 8.2 %all-to-all-start.6 = ((f32[32,16,512]{2,1,0:T(8,128)}), f32[32,16,512]{2,1,0:T(8,128)S(1)}, u32[]{:S(2)}, u32[]{:S(2)}) async-start(f32[32,16,512]{2,1,0:T(8,128)} %copy.102), calls=%async_computation.6 | async-start | bytes 2097152 | tf_op jit(solution)/shard_map/all_to_all | solution.py:52
  256.3 3.6 fusion.57
  259.8 36.8 %all-to-all-done.6 = f32[32,16,512]{2,1,0:T(8,128)S(1)} async-done(((f32[32,16,512]{2,1,0:T(8,128)}), f32[32,16,512]{2,1,0:T(8,128)S(1)}, u32[]{:S(2)}, u32[]{:S(2)}) %all-to-all-start.6) | async-done | bytes 1048608 | tf_op jit(solution)/shard_map/all_to_all | solution.py:52
  312.9 8.2 %all-to-all-start.8 = ((f32[2,256,256]{2,0,1:T(2,128)}), f32[2,256,256]{2,0,1:T(2,128)}, u32[]{:S(2)}, u32[]{:S(2)}) async-start(f32[2,256,256]{2,0,1:T(2,128)} %copy.112), calls=%async_computation.8 | async-start | bytes 1048576 | tf_op jit(solution)/shard_map/all_to_all | solution.py:73
  325.2 25.1 %all-to-all-done.8 = f32[2,256,256]{2,0,1:T(2,128)} async-done(((f32[2,256,256]{2,0,1:T(2,128)}), f32[2,256,256]{2,0,1:T(2,128)}, u32[]{:S(2)}, u32[]{:S(2)}) %all-to-all-start.8) | async-done | bytes 524320 | tf_op jit(solution)/shard_map/all_to_all | solution.py:73
  350.3 6.4 %all-to-all-start.9 = ((f32[2,256,256]{2,0,1:T(2,128)}), f32[2,256,256]{2,0,1:T(2,128)S(1)}, u32[]{:S(2)}, u32[]{:S(2)}) async-start(f32[2,256,256]{2,0,1:T(2,128)} %copy.115), calls=%async_computation.9 | async-start | bytes 1048576 | tf_op jit(solution)/shard_map/all_to_all | solution.py:74
  360.4 25.5 %all-to-all-done.9 = f32[2,256,256]{2,0,1:T(2,128)S(1)} async-done(((f32[2,256,256]{2,0,1:T(2,128)}), f32[2,256,256]{2,0,1:T(2,128)S(1)}, u32[]{:S(2)}, u32[]{:S(2)}) %all-to-all-start.9) | async-done | bytes 524320 | tf_op jit(solution)/shard_map/all_to_all | solution.py:74
  390.4 6.5 %all-to-all-start.10 = ((f32[16,16,256]{2,1,0:T(8,128)}), f32[16,16,256]{2,1,0:T(8,128)S(1)}, u32[]{:S(2)}, u32[]{:S(2)}) async-start(f32[16,16,256]{2,1,0:T(8,128)} %copy.118), calls=%async_computation.10 | async-start | bytes 524288 | tf_op jit(solution)/shard_map/all_to_all | solution.py:138
  397.5 17.8 %all-to-all-done.10 = f32[16,16,256]{2,1,0:T(8,128)S(1)} async-done(((f32[16,16,256]{2,1,0:T(8,128)}), f32[16,16,256]{2,1,0:T(8,128)S(1)}, u32[]{:S(2)}, u32[]{:S(2)}) %all-to-all-start.10) | async-done | bytes 262176 | tf_op jit(solution)/shard_map/all_to_all | solution.py:138
  415.4 24.1 %all_to_all.219 = f32[16,16,256]{2,1,0:T(8,128)S(1)} all-to-all(f32[16,16,256]{2,1,0:T(8,128)S(1)} %bitcast.184), channel_id=1, replica_groups=mesh['batch'=32,'seq'=16] {'seq'}, dimensions={0} | all-to-all | bytes 524288 | tf_op jit(solution)/shard_map/all_to_all | solution.py:127
  442.2 5.7 all-to-all-start.12
  449.1 28.0 %all-to-all-done.12 = f32[32,16,256]{2,1,0:T(8,128)} async-done(((f32[32,16,256]{2,1,0:T(8,128)}), f32[32,16,256]{2,1,0:T(8,128)}, u32[]{:S(2)}, u32[]{:S(2)}) %all-to-all-start.12) | async-done | bytes 524320 | tf_op jit(solution)/shard_map/all_to_all | solution.py:52
  477.1 6.5 %all-to-all-start.13 = ((f32[32,16,256]{2,1,0:T(8,128)}), f32[32,16,256]{2,1,0:T(8,128)S(1)}, u32[]{:S(2)}, u32[]{:S(2)}) async-start(f32[32,16,256]{2,1,0:T(8,128)} %copy.124), calls=%async_computation.13 | async-start | bytes 1048576 | tf_op jit(solution)/shard_map/all_to_all | solution.py:53
  487.3 25.3 %all-to-all-done.13 = f32[32,16,256]{2,1,0:T(8,128)S(1)} async-done(((f32[32,16,256]{2,1,0:T(8,128)}), f32[32,16,256]{2,1,0:T(8,128)S(1)}, u32[]{:S(2)}, u32[]{:S(2)}) %all-to-all-start.13) | async-done | bytes 524320 | tf_op jit(solution)/shard_map/all_to_all | solution.py:53
  522.4 6.7 %all-to-all-start.14 = ((f32[2,256,256]{2,0,1:T(2,128)}), f32[2,256,256]{2,0,1:T(2,128)S(1)}, u32[]{:S(2)}, u32[]{:S(2)}) async-start(f32[2,256,256]{2,0,1:T(2,128)} %copy.129), calls=%async_computation.14 | async-start | bytes 1048576 | tf_op jit(solution)/shard_map/all_to_all | solution.py:73
  533.3 24.9 %all-to-all-done.14 = f32[2,256,256]{2,0,1:T(2,128)S(1)} async-done(((f32[2,256,256]{2,0,1:T(2,128)}), f32[2,256,256]{2,0,1:T(2,128)S(1)}, u32[]{:S(2)}, u32[]{:S(2)}) %all-to-all-start.14) | async-done | bytes 524320 | tf_op jit(solution)/shard_map/all_to_all | solution.py:73
  558.1 6.3 %all-to-all-start.15 = ((f32[2,256,256]{2,0,1:T(2,128)}), f32[2,256,256]{2,0,1:T(2,128)S(1)}, u32[]{:S(2)}, u32[]{:S(2)}) async-start(f32[2,256,256]{2,0,1:T(2,128)} %copy.132), calls=%async_computation.15 | async-start | bytes 1048576 | tf_op jit(solution)/shard_map/all_to_all | solution.py:74
  565.3 28.2 %all-to-all-done.15 = f32[2,256,256]{2,0,1:T(2,128)S(1)} async-done(((f32[2,256,256]{2,0,1:T(2,128)}), f32[2,256,256]{2,0,1:T(2,128)S(1)}, u32[]{:S(2)}, u32[]{:S(2)}) %all-to-all-start.15) | async-done | bytes 524320 | tf_op jit(solution)/shard_map/all_to_all | solution.py:74
  595.6 24.5 %all_to_all.220 = f32[16,16,256]{2,1,0:T(8,128)S(1)} all-to-all(f32[16,16,256]{2,1,0:T(8,128)S(1)} %copy.135), channel_id=1, replica_groups=mesh['batch'=32,'seq'=16] {'seq'}, dimensions={0} | all-to-all | bytes 524288 | tf_op jit(solution)/shard_map/all_to_all | solution.py:138
  (140 shorter events, 99.8 us)
Async XLA Ops:
  0.0 52.7 %copy-start = (bf16[256,768]{1,0:T(8,128)(2,1)S(1)}, bf16[256,768]{1,0:T(8,128)(2,1)}, u32[]{:S(2)}) copy-start(bf16[256,768]{1,0:T(8,128)(2,1)} %param.14) | copy-start | bytes 1179652
  3.9 17.9 %copy-start.1 = (bf16[256,256]{1,0:T(8,128)(2,1)S(1)}, bf16[256,256]{1,0:T(8,128)(2,1)}, u32[]{:S(2)}) copy-start(bf16[256,256]{1,0:T(8,128)(2,1)} %param.8) | copy-start | bytes 393220
  6.6 27.6 %all-to-all-start.1 = ((s32[16,1,16]{2,1,0:T(1,128)}), s32[16,1,16]{2,1,0:T(1,128)S(1)}, u32[]{:S(2)}, u32[]{:S(2)}) async-start(s32[16,1,16]{2,1,0:T(1,128)} %all_to_all.155), calls=%async_computation.1 | async-start | bytes 16384 | tf_op jit(solution)/shard_map/all_to_all | solution.py:98
  34.1 17.4 %all-to-all-start = ((bf16[16,16,256]{2,1,0:T(8,128)(2,1)}), bf16[16,16,256]{2,1,0:T(8,128)(2,1)S(1)}, u32[]{:S(2)}, u32[]{:S(2)}) async-start(bf16[16,16,256]{2,1,0:T(8,128)(2,1)} %bitcast.1), calls=%async_computation | async-start | bytes 262144 | tf_op jit(solution)/shard_map/all_to_all | solution.py:97
  52.7 3.1 copy-start.21
  53.0 4.1 collective-permute-start
  57.4 6.9 %copy-start.19 = (f32[256,2,256]{2,1,0:T(2,128)S(1)}, f32[256,2,256]{2,1,0:T(2,128)}, u32[]{:S(2)}) copy-start(f32[256,2,256]{2,1,0:T(2,128)} %param.11) | copy-start | bytes 1572868
  58.1 22.7 %all-to-all-start.2 = ((f32[16,16,256]{2,1,0:T(8,128)}), f32[16,16,256]{2,1,0:T(8,128)S(1)}, u32[]{:S(2)}, u32[]{:S(2)}) async-start(f32[16,16,256]{2,1,0:T(8,128)} %bitcast.4), calls=%async_computation.2 | async-start | bytes 524288 | tf_op jit(solution)/shard_map/all_to_all | solution.py:127
  80.8 30.6 %all-to-all-start.5 = ((f32[16,16,512]{2,1,0:T(8,128)}), f32[16,16,512]{2,1,0:T(8,128)S(1)}, u32[]{:S(2)}, u32[]{:S(2)}) async-start(f32[16,16,512]{2,1,0:T(8,128)} %reshape.93), calls=%async_computation.5 | async-start | bytes 1048576 | tf_op jit(solution)/shard_map/all_to_all | solution.py:115
  111.4 34.6 %all-to-all-start.3 = ((f32[32,16,256]{2,1,0:T(8,128)}), f32[32,16,256]{2,1,0:T(8,128)S(1)}, u32[]{:S(2)}, u32[]{:S(2)}) async-start(f32[32,16,256]{2,1,0:T(8,128)} %copy.94), calls=%async_computation.3 | async-start | bytes 1048576 | tf_op jit(solution)/shard_map/all_to_all | solution.py:52
  146.0 9.8 %copy-start.16 = (f32[32,16,256]{2,1,0:T(8,128)}, f32[32,16,256]{2,1,0:T(8,128)S(1)}, u32[]{:S(2)}) copy-start(f32[32,16,256]{2,1,0:T(8,128)S(1)} %all-to-all-done.3) | copy-start | bytes 1572868
  146.0 35.5 %all-to-all-start.4 = ((f32[32,16,256]{2,1,0:T(8,128)}), f32[32,16,256]{2,1,0:T(8,128)}, u32[]{:S(2)}, u32[]{:S(2)}) async-start(f32[32,16,256]{2,1,0:T(8,128)} %copy.97), calls=%async_computation.4 | async-start | bytes 1048576 | tf_op jit(solution)/shard_map/all_to_all | solution.py:53
  181.6 56.1 %all-to-all-start.7 = ((f32[32,16,512]{2,1,0:T(8,128)}), f32[32,16,512]{2,1,0:T(8,128)S(1)}, u32[]{:S(2)}, u32[]{:S(2)}) async-start(f32[32,16,512]{2,1,0:T(8,128)} %copy.105), calls=%async_computation.7 | async-start | bytes 2097152 | tf_op jit(solution)/shard_map/all_to_all | solution.py:53
  238.6 58.1 %all-to-all-start.6 = ((f32[32,16,512]{2,1,0:T(8,128)}), f32[32,16,512]{2,1,0:T(8,128)S(1)}, u32[]{:S(2)}, u32[]{:S(2)}) async-start(f32[32,16,512]{2,1,0:T(8,128)} %copy.102), calls=%async_computation.6 | async-start | bytes 2097152 | tf_op jit(solution)/shard_map/all_to_all | solution.py:52
  253.6 2.6 copy-start.6
  296.8 2.6 copy-start.4
  302.4 2.7 copy-start.7
  302.4 2.7 copy-start.13
  302.4 2.7 copy-start.17
  305.1 1.9 copy-start.2
  312.9 37.4 %all-to-all-start.8 = ((f32[2,256,256]{2,0,1:T(2,128)}), f32[2,256,256]{2,0,1:T(2,128)}, u32[]{:S(2)}, u32[]{:S(2)}) async-start(f32[2,256,256]{2,0,1:T(2,128)} %copy.112), calls=%async_computation.8 | async-start | bytes 1048576 | tf_op jit(solution)/shard_map/all_to_all | solution.py:73
  350.3 35.6 %all-to-all-start.9 = ((f32[2,256,256]{2,0,1:T(2,128)}), f32[2,256,256]{2,0,1:T(2,128)S(1)}, u32[]{:S(2)}, u32[]{:S(2)}) async-start(f32[2,256,256]{2,0,1:T(2,128)} %copy.115), calls=%async_computation.9 | async-start | bytes 1048576 | tf_op jit(solution)/shard_map/all_to_all | solution.py:74
  390.4 6.5 %copy-start.23 = (f32[2,256]{1,0:T(2,128)S(1)}, f32[2,256]{1,0:T(2,128)}, u32[]{:S(2)}) copy-start(f32[2,256]{1,0:T(2,128)} %param.12) | copy-start | bytes 6148
  390.4 24.9 %all-to-all-start.10 = ((f32[16,16,256]{2,1,0:T(8,128)}), f32[16,16,256]{2,1,0:T(8,128)S(1)}, u32[]{:S(2)}, u32[]{:S(2)}) async-start(f32[16,16,256]{2,1,0:T(8,128)} %copy.118), calls=%async_computation.10 | async-start | bytes 524288 | tf_op jit(solution)/shard_map/all_to_all | solution.py:138
  442.2 34.8 %all-to-all-start.12 = ((f32[32,16,256]{2,1,0:T(8,128)}), f32[32,16,256]{2,1,0:T(8,128)}, u32[]{:S(2)}, u32[]{:S(2)}) async-start(f32[32,16,256]{2,1,0:T(8,128)} %copy.121), calls=%async_computation.12 | async-start | bytes 1048576 | tf_op jit(solution)/shard_map/all_to_all | solution.py:52
  477.1 35.5 %all-to-all-start.13 = ((f32[32,16,256]{2,1,0:T(8,128)}), f32[32,16,256]{2,1,0:T(8,128)S(1)}, u32[]{:S(2)}, u32[]{:S(2)}) async-start(f32[32,16,256]{2,1,0:T(8,128)} %copy.124), calls=%async_computation.13 | async-start | bytes 1048576 | tf_op jit(solution)/shard_map/all_to_all | solution.py:53
  484.6 2.6 copy-start.14
  514.5 1.9 copy-start.3
  514.5 1.9 copy-start.15
  522.4 6.7 %copy-start.11 = (f32[2,256,256]{1,2,0:T(8,128)S(1)}, f32[2,256,256]{1,2,0:T(8,128)}, u32[]{:S(2)}) copy-start(f32[2,256,256]{1,2,0:T(8,128)} %copy-done.10) | copy-start | bytes 1572868
  522.4 35.7 %all-to-all-start.14 = ((f32[2,256,256]{2,0,1:T(2,128)}), f32[2,256,256]{2,0,1:T(2,128)S(1)}, u32[]{:S(2)}, u32[]{:S(2)}) async-start(f32[2,256,256]{2,0,1:T(2,128)} %copy.129), calls=%async_computation.14 | async-start | bytes 1048576 | tf_op jit(solution)/shard_map/all_to_all | solution.py:73
  558.1 35.4 %all-to-all-start.15 = ((f32[2,256,256]{2,0,1:T(2,128)}), f32[2,256,256]{2,0,1:T(2,128)S(1)}, u32[]{:S(2)}, u32[]{:S(2)}) async-start(f32[2,256,256]{2,0,1:T(2,128)} %copy.132), calls=%async_computation.15 | async-start | bytes 1048576 | tf_op jit(solution)/shard_map/all_to_all | solution.py:74
  (8 other events, 10.4 us)
where the time goes:
time: 633 us; the launch traced here: 623 us
  waiting for transfers between devices  368 us (58%)
  starting transfers between devices  109 us (17%)
  matrix products  50.9 us (8%)
  blocking collectives  48.6 us (8%)
  local copies, waits for them, and re-layouts  36.5 us (6%)
  other arithmetic  8.36 us (1%)
    all_to_all x3, waiting for transfers between devices, forward(): lax.all_to_all(twist_imag, 'seq', split_axis=0, concat_axis=1, tiled=True)  97.4 us
    all_to_all x3, waiting for transfers between devices, forward(): lax.all_to_all(twist_real, 'seq', split_axis=0, concat_axis=1, tiled=True)  90.8 us
    all_to_all x2, waiting for transfers between devices, inverse(): lax.all_to_all(back_imag, 'seq', split_axis=1, concat_axis=0, tiled=True)  53.7 us
    all_to_all x2, waiting for transfers between devices, inverse(): lax.all_to_all(back_real, 'seq', split_axis=1, concat_axis=0, tiled=True)  50 us
    dot_general x30, matrix products, product(): return jnp.einsum(form, left, right, precision=lax.Precision.HIGHEST)  49.8 us
    all_to_all x1, blocking collectives, convolve(): lax.all_to_all(result, 'seq', split_axis=0, concat_axis=0, tiled=True)  24.5 us
    all_to_all x1, blocking collectives, convolve(): lax.all_to_all(signal.reshape(dev_count, col_size, features), 'seq', spli...  24.1 us
    all_to_all x1, waiting for transfers between devices, body(): lax.all_to_all(filters.reshape(dev_count, col_size, 2 * features), 'seq',...  22.7 us
  transfers between devices with their start and end apart: 16, of which 16 were waited for; matrix products, arithmetic and copies ran while one was open for 7% of the time, Pallas kernels for 0%

commit v1 on v0

v1 whole, which is shorter than its diff:
```python
import functools
import math

import jax
import jax.numpy as jnp
import ml_dtypes
import numpy as np
from jax import lax
from jax.experimental import pallas as pl
from jax.experimental.pallas import tpu as pltpu
from jax.sharding import PartitionSpec as P

N = 16
W = 256
POINTS = 2 * N * W
F32, BF16 = jnp.float32, jnp.bfloat16


def split(table):
    high = table.astype(ml_dtypes.bfloat16)
    low = (table - high.astype(np.float64)).astype(ml_dtypes.bfloat16)
    return high, low


@functools.cache
def make_tables():
    half = np.arange(N) + 0.5
    outer = 2 * np.pi * np.outer(half, np.arange(N)) / (2 * N)
    eye = np.eye(N)
    fwd_a = np.concatenate([np.kron(np.cos(outer), eye), np.kron(-np.sin(outer), eye)], 0)
    inv_a = np.concatenate([np.kron(np.cos(outer.T), eye), np.kron(-np.sin(outer.T), eye)], 1) * (2.0 / POINTS)
    inner = 2 * np.pi * (np.outer(np.arange(W), np.arange(W)) % W) / W
    cos, sin = np.cos(inner), np.sin(inner)
    fwd_b = np.block([[cos, -sin], [sin, cos]])
    inv_b = np.block([[cos, sin], [-sin, cos]])
    twist = 2 * np.pi * np.outer(half, np.arange(W)) / POINTS
    cat = lambda table, axis: np.concatenate([split(table)[i] for i in (0, 0, 1)], axis)
    return (
        cat(fwd_a, 1),
        cat(fwd_b, 0),
        cat(inv_b, 0),
        cat(inv_a, 1),
        np.stack([np.cos(twist), np.sin(twist)]).astype(np.float32),
    )


def parts(x, axis):
    high = x.astype(BF16)
    low = (x - high.astype(F32)).astype(BF16)
    return jnp.concatenate([high, low, high], axis=axis)


def dot(a, b, dims=((1,), (0,))):
    return lax.dot_general(a, b, (dims, ((), ())), preferred_element_type=F32)


def kernel(
    n_batch,
    length,
    positions,
    events,
    filters,
    skip_gain,
    short_filter,
    in_proj,
    out_proj,
    fwd_a_hbm,
    fwd_b_hbm,
    inv_b_hbm,
    inv_a_hbm,
    twist_hbm,
    out,
    fwd_a,
    fwd_b,
    inv_b,
    inv_a,
    twist,
    thirds,
    block_row,
    taps,
    gated,
    recv_sig,
    recv_blk,
    recv_tap,
    recv_out,
    spec,
    table_sem,
    sig_send,
    sig_recv,
    blk_send,
    blk_recv,
    tap_send,
    tap_recv,
    own_send,
    own_recv,
    out_send,
    out_recv,
):
    me = lax.axis_index("seq")
    lane = lax.axis_index("batch")
    column, core = lane // 2, lane % 2

    barrier = pltpu.get_barrier_semaphore()

    def greet(k, carry):
        pl.semaphore_signal(barrier, inc=1, device_id={"seq": (me + k) % N})
        return carry

    def greet_plane(k, carry):
        pl.semaphore_signal(barrier, inc=1, device_id={"batch": (lane + k) % n_batch})
        return carry

    lax.fori_loop(1, N, greet, 0)
    lax.fori_loop(1, n_batch, greet_plane, 0)

    tables = [
        pltpu.make_async_copy(src, dst, table_sem.at[i])
        for i, (src, dst) in enumerate(
            ((fwd_a_hbm, fwd_a), (twist_hbm, twist), (fwd_b_hbm, fwd_b), (inv_b_hbm, inv_b), (inv_a_hbm, inv_a))
        )
    ]
    for copy in tables:
        copy.start()

    target = (me + column) % N
    rows16 = lax.broadcasted_iota(jnp.int32, (N, W), 0)
    lanes16 = lax.broadcasted_iota(jnp.int32, (N, W), 1)
    pick = (lanes16 == rows16 + target * N).astype(BF16)
    lags = jnp.where(core == 0, filters[:, 0:W], filters[:, W : 2 * W]).astype(BF16)
    taps[...] = dot(pick, lags, ((1,), (1,))).astype(BF16)

    pos = positions[...]
    order = lax.broadcasted_iota(jnp.int32, (W, W), 0) == pos % W
    one_hot = order.astype(BF16)
    kept = jnp.where(pos < length[0], one_hot, jnp.zeros_like(one_hot))
    ids = jnp.broadcast_to((pos // W).astype(BF16), (N, W))
    block_row[...] = dot(ids, one_hot, ((1,), (1,)))[0:8].astype(jnp.int32)
    ordered = dot(kept, events[...]).astype(BF16)
    for t in range(3):
        projected = dot(ordered, in_proj[:, t * W : (t + 1) * W])
        thirds[t] = projected.T.astype(BF16).reshape(N, N, W)

    pl.semaphore_wait(barrier, N - 1 + n_batch - 1)

    def tap_first():
        return pltpu.make_async_remote_copy(
            src_ref=taps,
            dst_ref=recv_tap.at[core, me],
            send_sem=own_send,
            recv_sem=own_recv,
            device_id={"seq": target},
        )

    slot = (me + N - column) % N

    @pl.when(column != 0)
    def _():
        tap_first().start()

    @pl.when(column == 0)
    def _():
        recv_tap[core, me] = taps[...]

    def block_copy(k):
        peer = (me + k) % N
        return pltpu.make_async_remote_copy(
            src_ref=block_row,
            dst_ref=recv_blk.at[me],
            send_sem=blk_send.at[peer],
            recv_sem=blk_recv.at[me],
            device_id={"seq": peer},
        )

    def block_arrival(k):
        peer = (me + k) % N
        return pltpu.make_async_remote_copy(
            src_ref=block_row,
            dst_ref=recv_blk.at[peer],
            send_sem=blk_send.at[peer],
            recv_sem=blk_recv.at[peer],
            device_id={"seq": peer},
        )

    def third_copy(t, k):
        peer = (me + k) % N
        return pltpu.make_async_remote_copy(
            src_ref=thirds.at[t, peer],
            dst_ref=recv_sig.at[t, me],
            send_sem=sig_send.at[t, peer],
            recv_sem=sig_recv.at[t, me],
            device_id={"seq": peer},
        )

    def third_arrival(t, k):
        peer = (me + k) % N
        return pltpu.make_async_remote_copy(
            src_ref=thirds.at[t, peer],
            dst_ref=recv_sig.at[t, peer],
            send_sem=sig_send.at[t, peer],
            recv_sem=sig_recv.at[t, peer],
            device_id={"seq": peer},
        )

    def each(count, act):
        def step(k, carry):
            act(k)
            return carry

        lax.fori_loop(1, count, step, 0)

    each(N, lambda k: block_copy(k).start())
    for t in range(3):
        each(N, lambda k: third_copy(t, k).start())
    recv_blk[me] = block_row[...]
    for t in range(3):
        recv_sig[t, me] = thirds[t, me]

    @pl.when(column != 0)
    def _():
        pltpu.make_async_remote_copy(
            src_ref=taps,
            dst_ref=recv_tap.at[core, slot],
            send_sem=own_send,
            recv_sem=own_recv,
            device_id={"seq": target},
        ).wait_recv()

    def tap_copy(k):
        peer = (lane + k) % n_batch
        return pltpu.make_async_remote_copy(
            src_ref=recv_tap.at[core, slot],
            dst_ref=recv_tap.at[core, slot],
            send_sem=tap_send.at[peer],
            recv_sem=tap_recv.at[lane],
            device_id={"batch": peer},
        )

    def tap_arrival(k):
        peer = (lane + k) % n_batch
        there = recv_tap.at[peer % 2, (me + N - peer // 2) % N]
        return pltpu.make_async_remote_copy(
            src_ref=there,
            dst_ref=there,
            send_sem=tap_send.at[peer],
            recv_sem=tap_recv.at[peer],
            device_id={"batch": peer},
        )

    each(n_batch, lambda k: tap_copy(k).start())

    def column_of(row):
        return jnp.sum(jnp.where(lanes16 == rows16 + me * N, row, 0.0), axis=1, keepdims=True)[None]

    def rotate(re, im, sign):
        cos = twist[0][:, None, :]
        sin = twist[1][:, None, :] * sign
        re, im = re.reshape(N, N, W), im.reshape(N, N, W)
        return (re * cos + im * sin).reshape(W, W), (im * cos - re * sin).reshape(W, W)

    def forward(signal):
        mid = dot(fwd_a[...], parts(signal, 0))
        re, im = rotate(mid[:W], mid[W:], 1.0)
        return dot(parts(jnp.concatenate([re, im], axis=1), 1), fwd_b[...])

    def inverse(re, im):
        mid = dot(parts(jnp.concatenate([re, im], axis=1), 1), inv_b[...])
        re, im = rotate(mid[:, :W], mid[:, W:], -1.0)
        return dot(inv_a[...], parts(jnp.concatenate([re, im], axis=0), 0))

    def convolve(signal, f):
        got = forward(signal)
        re, im = got[:, :W], got[:, W:]
        tap_re, tap_im = spec[f, :, :W], spec[f, :, W:]
        return inverse(re * tap_re - im * tap_im, re * tap_im + im * tap_re)

    sub = lax.broadcasted_iota(jnp.int32, (W, W), 1)

    def short(t):
        rows = []
        got = [recv_sig[t, s].astype(F32) for s in range(N)]
        for b in range(N):
            total = jnp.zeros((N, W), F32)
            for s in range(N):
                row = jnp.concatenate([recv_blk[s, 0:1, :]], axis=0)
                total = jnp.where(row == b, got[s], total)
            rows.append(total)
        stream = jnp.concatenate(rows, axis=0)
        before = jnp.concatenate([jnp.zeros((N, W), F32), stream[:-N]], axis=0)
        one = pltpu.roll(jnp.where(sub == W - 1, before, stream), 1, 1)
        two = pltpu.roll(jnp.where(sub >= W - 2, before, stream), 2, 1)
        tap = [column_of(short_filter[i : i + 1, t * W : (t + 1) * W]) for i in range(3)]
        blocks = lambda x: x.reshape(N, N, W)
        return (tap[0] * blocks(stream) + tap[1] * blocks(one) + tap[2] * blocks(two)).reshape(W, W)

    for copy in tables:
        copy.wait()
    each(N, lambda k: block_arrival(k).wait_recv())
    each(n_batch, lambda k: tap_arrival(k).wait_recv())
    for f in range(2):
        spec[f] = forward(recv_tap[f].reshape(W, W).astype(F32))

    each(N, lambda k: third_arrival(0, k).wait_recv())
    value = short(0)
    gain = [column_of(skip_gain[i : i + 1, :]) for i in range(2)]
    scaled = lambda g, x: (g * x.reshape(N, N, W)).reshape(W, W)
    first = convolve(value, 0) + scaled(gain[0], value)
    each(N, lambda k: third_arrival(1, k).wait_recv())
    first = short(1) * first
    second = convolve(first, 1) + scaled(gain[1], first)
    each(N, lambda k: third_arrival(2, k).wait_recv())
    gated[...] = (short(2) * second).astype(BF16).reshape(N, N, W)

    def out_copy(k):
        peer = (me + k) % N
        return pltpu.make_async_remote_copy(
            src_ref=gated.at[peer],
            dst_ref=recv_out.at[me],
            send_sem=out_send.at[peer],
            recv_sem=out_recv.at[me],
            device_id={"seq": peer},
        )

    def out_arrival(k):
        peer = (me + k) % N
        return pltpu.make_async_remote_copy(
            src_ref=gated.at[peer],
            dst_ref=recv_out.at[peer],
            send_sem=out_send.at[peer],
            recv_sem=out_recv.at[peer],
            device_id={"seq": peer},
        )

    each(N, lambda k: out_copy(k).start())
    recv_out[me] = gated[me]

    @pl.when(column != 0)
    def _():
        tap_first().wait_send()

    each(N, lambda k: block_copy(k).wait_send())
    for t in range(3):
        each(N, lambda k: third_copy(t, k).wait_send())
    each(n_batch, lambda k: tap_copy(k).wait_send())
    each(N, lambda k: out_copy(k).wait_send())
    each(N, lambda k: out_arrival(k).wait_recv())
    whole = recv_out[...].reshape(W, W)
    out[...] = dot(whole, out_proj[...], ((0,), (0,))).astype(BF16)


def body(n_batch, events, positions, length, filters, skip_gain, short_filter, in_proj, out_proj):
    tables = [jnp.asarray(table) for table in make_tables()]
    vmem, smem, anywhere = (pl.BlockSpec(memory_space=m) for m in (pltpu.VMEM, pltpu.SMEM, pl.ANY))
    dma = lambda *shape: pltpu.SemaphoreType.DMA(shape)
    return pl.pallas_call(
        functools.partial(kernel, n_batch),
        out_shape=jax.ShapeDtypeStruct((W, W), BF16),
        in_specs=[smem] + [vmem] * 7 + [anywhere] * 5,
        out_specs=vmem,
        scratch_shapes=[pltpu.VMEM(table.shape, table.dtype) for table in tables]
        + [
            pltpu.VMEM((3, N, N, W), BF16),
            pltpu.VMEM((8, W), jnp.int32),
            pltpu.VMEM((N, W), BF16),
            pltpu.VMEM((N, N, W), BF16),
            pltpu.VMEM((3, N, N, W), BF16),
            pltpu.VMEM((N, 8, W), jnp.int32),
            pltpu.VMEM((2, N, N, W), BF16),
            pltpu.VMEM((N, N, W), BF16),
            pltpu.VMEM((2, W, 2 * W), F32),
            dma(5),
            dma(3, N),
            dma(3, N),
            dma(N),
            dma(N),
            dma(n_batch),
            dma(n_batch),
            pltpu.SemaphoreType.DMA,
            pltpu.SemaphoreType.DMA,
            dma(N),
            dma(N),
        ],
        compiler_params=pltpu.CompilerParams(
            collective_id=0, has_side_effects=True, vmem_limit_bytes=48 * 1024 * 1024
        ),
    )(
        length,
        positions.reshape(1, W),
        events,
        filters.reshape(W, 2 * W),
        skip_gain,
        short_filter,
        in_proj,
        out_proj,
        *tables,
    )


def solution(mesh):
    return jax.shard_map(
        functools.partial(body, mesh.shape["batch"]),
        mesh=mesh,
        in_specs=(
            P(("batch", "seq"), None),
            P(("batch", "seq")),
            P("batch"),
            P("seq", None, None),
            P(),
            P(),
            P(),
            P(),
        ),
        out_specs=P(("batch", "seq"), None),
        check_vma=False,
    )
```

time: 633 us -> 69.6 us (0.11)
  the two profiles are of different devices: /device:TPU:6 before, /device:TPU:14 now
where the time goes in v1:
time: 69.6 us; the launch traced here: 69.1 us
  Pallas kernels  57 us (82%)
  local copies, waits for them, and re-layouts  11.3 us (16%)
  between operations  0.76 us (1%)
    pallas_call x1, Pallas kernels, body(): pl.pallas_call(functools.partial(kernel, n_batch), out_shape=jax.ShapeDty...  57 us
    unnamed x24, local copies, waits for them, and re-layouts  11.3 us

profile of v1, /device:TPU:14, one launch (start us, length us, event | category | flops | bytes accessed | tf_op | source)
XLA Modules:
  0.0 69.1 jit_solution(6722321687818629382)
XLA Ops:
  0.0 0.0 copy-start.2
  0.7 1.1 %copy.14 = f32[32,8,2,256]{3,1,2,0:T(8,128)S(1)} copy(f32[32,8,2,256]{3,2,1,0:T(2,128)} %bitcast.5) | data formatting | bytes 1048576
  1.8 0.0 copy-done.2
  1.8 0.0 copy-start
  1.8 1.4 %copy-done = bf16[1536,512]{1,0:T(8,128)(2,1)S(1)} copy-done((bf16[1536,512]{1,0:T(8,128)(2,1)S(1)}, bf16[1536,512]{1,0:T(8,128)(2,1)}, u32[]{:S(2)}) %copy-start) | copy-done | bytes 1572888
  3.2 0.0 copy-start.1
  3.2 1.4 %copy-done.1 = bf16[1536,512]{1,0:T(8,128)(2,1)S(1)} copy-done((bf16[1536,512]{1,0:T(8,128)(2,1)S(1)}, bf16[1536,512]{1,0:T(8,128)(2,1)}, u32[]{:S(2)}) %copy-start.1) | copy-done | bytes 1572888
  4.6 0.0 copy-start.3
  4.6 1.1 %copy-done.3 = bf16[512,768]{1,0:T(8,128)(2,1)S(1)} copy-done((bf16[512,768]{1,0:T(8,128)(2,1)S(1)}, bf16[512,768]{1,0:T(8,128)(2,1)}, u32[]{:S(2)}) %copy-start.3) | copy-done | bytes 786456
  5.8 0.0 copy-start.4
  5.8 1.0 %copy-done.4 = bf16[256,768]{1,0:T(8,128)(2,1)S(1)} copy-done((bf16[256,768]{1,0:T(8,128)(2,1)S(1)}, bf16[256,768]{1,0:T(8,128)(2,1)}, u32[]{:S(2)}) %copy-start.4) | copy-done | bytes 393240
  6.8 0.0 copy-start.5
  6.8 0.9 %copy-done.5 = bf16[256,256]{1,0:T(8,128)(2,1)S(1)} copy-done((bf16[256,256]{1,0:T(8,128)(2,1)S(1)}, bf16[256,256]{1,0:T(8,128)(2,1)}, u32[]{:S(2)}) %copy-start.5) | copy-done | bytes 131096
  7.7 0.0 copy-start.6
  7.7 0.9 %copy-done.6 = bf16[256,256]{1,0:T(8,128)(2,1)S(1)} copy-done((bf16[256,256]{1,0:T(8,128)(2,1)S(1)}, bf16[256,256]{1,0:T(8,128)(2,1)}, u32[]{:S(2)}) %copy-start.6) | copy-done | bytes 131096
  8.6 0.0 copy-start.7
  8.6 0.8 %copy-done.7 = f32[2,16,256]{2,1,0:T(8,128)S(1)} copy-done((f32[2,16,256]{2,1,0:T(8,128)S(1)}, f32[2,16,256]{2,1,0:T(8,128)}, u32[]{:S(2)}) %copy-start.7) | copy-done | bytes 32792
  9.3 0.0 copy-start.8
  9.3 0.7 %copy-done.8 = f32[3,768]{1,0:T(4,128)S(1)} copy-done((f32[3,768]{1,0:T(4,128)S(1)}, f32[3,768]{1,0:T(4,128)}, u32[]{:S(2)}) %copy-start.8) | copy-done | bytes 9240
  10.0 0.0 copy-start.9
  10.0 0.7 copy-done.9
  10.7 0.0 copy-start.10
  10.7 0.7 copy-done.10
  11.4 57.0 %shard_map.127 = bf16[256,256]{1,0:T(8,128)(2,1)S(1)} custom-call(s32[1]{0:T(128)S(6)} %copy.16.length, s32[1,256]{1,0:T(1,128)S(1)} %bitcast.4, bf16[256,256]{1,0:T(8,128)(2,1)S(1)} %copy-done.5, f32[256,512]{1,0:T(8,128)S(1)} %bitcast.3, f32[2,256]{1,0:T(2,128)S(1)} %copy-done.9, f32[3,768]{1,0:T(4,128)S(1)} %copy-done.8, bf16[256,768]{1,0:T(8,128)(2,1)S(1)} %copy-done.4, ...), custom_call_target="tpu_custom_call" | custom-call | tf_op jit(solution)/shard_map/pallas_call | solution.py:354
  68.4 0.7 copy.17
Async XLA Ops:
  0.0 1.8 %copy-start.2 = (bf16[256,1536]{1,0:T(8,128)(2,1)S(1)}, bf16[256,1536]{1,0:T(8,128)(2,1)}, u32[]{:S(2)}) copy-start(bf16[256,1536]{1,0:T(8,128)(2,1)} %constant.13.clone.inv_a_hbm) | copy-start | bytes 2359300
  1.8 1.4 %copy-start = (bf16[1536,512]{1,0:T(8,128)(2,1)S(1)}, bf16[1536,512]{1,0:T(8,128)(2,1)}, u32[]{:S(2)}) copy-start(bf16[1536,512]{1,0:T(8,128)(2,1)} %constant.12.clone.inv_b_hbm) | copy-start | bytes 4718596
  3.2 1.4 %copy-start.1 = (bf16[1536,512]{1,0:T(8,128)(2,1)S(1)}, bf16[1536,512]{1,0:T(8,128)(2,1)}, u32[]{:S(2)}) copy-start(bf16[1536,512]{1,0:T(8,128)(2,1)} %constant.11.clone.fwd_b_hbm) | copy-start | bytes 4718596
  4.6 1.1 %copy-start.3 = (bf16[512,768]{1,0:T(8,128)(2,1)S(1)}, bf16[512,768]{1,0:T(8,128)(2,1)}, u32[]{:S(2)}) copy-start(bf16[512,768]{1,0:T(8,128)(2,1)} %constant.10.clone.fwd_a_hbm) | copy-start | bytes 2359300
  5.8 1.0 %copy-start.4 = (bf16[256,768]{1,0:T(8,128)(2,1)S(1)}, bf16[256,768]{1,0:T(8,128)(2,1)}, u32[]{:S(2)}) copy-start(bf16[256,768]{1,0:T(8,128)(2,1)} %in_proj.1) | copy-start | bytes 1179652
  6.8 0.9 %copy-start.5 = (bf16[256,256]{1,0:T(8,128)(2,1)S(1)}, bf16[256,256]{1,0:T(8,128)(2,1)}, u32[]{:S(2)}) copy-start(bf16[256,256]{1,0:T(8,128)(2,1)} %events.1) | copy-start | bytes 393220
  7.7 0.9 %copy-start.6 = (bf16[256,256]{1,0:T(8,128)(2,1)S(1)}, bf16[256,256]{1,0:T(8,128)(2,1)}, u32[]{:S(2)}) copy-start(bf16[256,256]{1,0:T(8,128)(2,1)} %out_proj.1) | copy-start | bytes 393220
  8.6 0.8 %copy-start.7 = (f32[2,16,256]{2,1,0:T(8,128)S(1)}, f32[2,16,256]{2,1,0:T(8,128)}, u32[]{:S(2)}) copy-start(f32[2,16,256]{2,1,0:T(8,128)} %constant.14.clone.twist_hbm) | copy-start | bytes 98308
  9.3 0.7 %copy-start.8 = (f32[3,768]{1,0:T(4,128)S(1)}, f32[3,768]{1,0:T(4,128)}, u32[]{:S(2)}) copy-start(f32[3,768]{1,0:T(4,128)} %short_filter.1) | copy-start | bytes 27652
  10.0 0.7 copy-start.9
  10.7 0.7 copy-start.10

commit v2 on v1

--- a/solution.py
+++ b/solution.py
@@ -54,52 +54,48 @@
     return lax.dot_general(a, b, (dims, ((), ())), preferred_element_type=F32)
 
 
-def kernel(
-    n_batch,
-    length,
-    positions,
-    events,
-    filters,
-    skip_gain,
-    short_filter,
-    in_proj,
-    out_proj,
-    fwd_a_hbm,
-    fwd_b_hbm,
-    inv_b_hbm,
-    inv_a_hbm,
-    twist_hbm,
-    out,
-    fwd_a,
-    fwd_b,
-    inv_b,
-    inv_a,
-    twist,
-    thirds,
-    block_row,
-    taps,
-    gated,
-    recv_sig,
-    recv_blk,
-    recv_tap,
-    recv_out,
-    spec,
-    table_sem,
-    sig_send,
-    sig_recv,
-    blk_send,
-    blk_recv,
-    tap_send,
-    tap_recv,
-    own_send,
-    own_recv,
-    out_send,
-    out_recv,
-):
+INPUTS = 13
+
+
+def kernel(n_batch, *refs):
+    outside, (out, *inside), rest = refs[:INPUTS], refs[INPUTS : 2 * INPUTS + 1], refs[2 * INPUTS + 1 :]
+    length, positions, events, filters, skip_gain, short_filter, in_proj, out_proj, *tables = inside
+    fwd_a, fwd_b, inv_b, inv_a, twist = tables
+    (
+        thirds,
+        block_row,
+        taps,
+        gated,
+        recv_sig,
+        recv_blk,
+        recv_tap,
+        recv_out,
+        spec,
+        load_sem,
+        sig_send,
+        sig_recv,
+        blk_send,
+        blk_recv,
+        tap_send,
+        tap_recv,
+        own_send,
+        own_recv,
+        out_send,
+        out_recv,
+    ) = rest
     me = lax.axis_index("seq")
     lane = lax.axis_index("batch")
     column, core = lane // 2, lane % 2
 
+    target = (me + column) % N
+    loads = []
+    for i, (src, dst) in enumerate(zip(outside, inside)):
+        if i == 3:
+            src = src.at[:, :, pl.ds(pl.multiple_of(target // 8 * 128, 128), 128)]
+        loads.append(pltpu.make_async_copy(src, dst, load_sem.at[i]))
+    for i in (1, 2, 6, 0, 3, 8, 12, 9, 5, 4, 10, 11, 7):
+        loads[i].start()
+
     barrier = pltpu.get_barrier_semaphore()
 
     def greet(k, carry):
@@ -113,34 +109,25 @@
     lax.fori_loop(1, N, greet, 0)
     lax.fori_loop(1, n_batch, greet_plane, 0)
 
-    tables = [
-        pltpu.make_async_copy(src, dst, table_sem.at[i])
-        for i, (src, dst) in enumerate(
-            ((fwd_a_hbm, fwd_a), (twist_hbm, twist), (fwd_b_hbm, fwd_b), (inv_b_hbm, inv_b), (inv_a_hbm, inv_a))
-        )
-    ]
-    for copy in tables:
-        copy.start()
-
-    target = (me + column) % N
-    rows16 = lax.broadcasted_iota(jnp.int32, (N, W), 0)
-    lanes16 = lax.broadcasted_iota(jnp.int32, (N, W), 1)
-    pick = (lanes16 == rows16 + target * N).astype(BF16)
-    lags = jnp.where(core == 0, filters[:, 0:W], filters[:, W : 2 * W]).astype(BF16)
-    taps[...] = dot(pick, lags, ((1,), (1,))).astype(BF16)
-
+    for i in (1, 0, 2, 6):
+        loads[i].wait()
     pos = positions[...]
     order = lax.broadcasted_iota(jnp.int32, (W, W), 0) == pos % W
     one_hot = order.astype(BF16)
-    kept = jnp.where(pos < length[0], one_hot, jnp.zeros_like(one_hot))
+    kept = jnp.where(pos < length[...], one_hot, jnp.zeros_like(one_hot))
     ids = jnp.broadcast_to((pos // W).astype(BF16), (N, W))
-    block_row[...] = dot(ids, one_hot, ((1,), (1,)))[0:8].astype(jnp.int32)
+    block_row[...] = dot(ids, one_hot, ((1,), (1,)))[0:1].astype(jnp.int32)
     ordered = dot(kept, events[...]).astype(BF16)
-    for t in range(3):
+
+    def project(t):
         projected = dot(ordered, in_proj[:, t * W : (t + 1) * W])
         thirds[t] = projected.T.astype(BF16).reshape(N, N, W)
 
+    project(0)
     pl.semaphore_wait(barrier, N - 1 + n_batch - 1)
+
+    rows16 = lax.broadcasted_iota(jnp.int32, (N, W), 0)
+    lanes16 = lax.broadcasted_iota(jnp.int32, (N, W), 1)
 
     def tap_first():
         return pltpu.make_async_remote_copy(
@@ -153,14 +140,6 @@
 
     slot = (me + N - column) % N
 
-    @pl.when(column != 0)
-    def _():
-        tap_first().start()
-
-    @pl.when(column == 0)
-    def _():
-        recv_tap[core, me] = taps[...]
-
     def block_copy(k):
         peer = (me + k) % N
         return pltpu.make_async_remote_copy(
@@ -209,10 +188,26 @@
         lax.fori_loop(1, count, step, 0)
 
     each(N, lambda k: block_copy(k).start())
-    for t in range(3):
+    each(N, lambda k: third_copy(0, k).start())
+    recv_blk[me] = block_row[...]
+    recv_sig[0, me] = thirds[0, me]
+
+    loads[3].wait()
+    pick = (lanes16[:, :128] == rows16[:, :128] + target % 8 * N).astype(BF16)
+    lags = jnp.where(core == 0, filters[:, 0, :], filters[:, 1, :]).astype(BF16)
+    taps[...] = dot(pick, lags, ((1,), (1,))).astype(BF16)
+
+    @pl.when(column != 0)
+    def _():
+        tap_first().start()
+
+    @pl.when(column == 0)
+    def _():
+        recv_tap[core, me] = taps[...]
+
+    for t in (1, 2):
+        project(t)
         each(N, lambda k: third_copy(t, k).start())
-    recv_blk[me] = block_row[...]
-    for t in range(3):
         recv_sig[t, me] = thirds[t, me]
 
     @pl.when(column != 0)
@@ -281,8 +276,7 @@
         for b in range(N):
             total = jnp.zeros((N, W), F32)
             for s in range(N):
-                row = jnp.concatenate([recv_blk[s, 0:1, :]], axis=0)
-                total = jnp.where(row == b, got[s], total)
+                total = jnp.where(recv_blk[s] == b, got[s], total)
             rows.append(total)
         stream = jnp.concatenate(rows, axis=0)
         before = jnp.concatenate([jnp.zeros((N, W), F32), stream[:-N]], axis=0)
@@ -292,8 +286,8 @@
         blocks = lambda x: x.reshape(N, N, W)
         return (tap[0] * blocks(stream) + tap[1] * blocks(one) + tap[2] * blocks(two)).reshape(W, W)
 
-    for copy in tables:
-        copy.wait()
+    for i in (8, 12, 9, 5, 4, 10, 11, 7):
+        loads[i].wait()
     each(N, lambda k: block_arrival(k).wait_recv())
     each(n_batch, lambda k: tap_arrival(k).wait_recv())
     for f in range(2):
@@ -349,25 +343,36 @@
 
 def body(n_batch, events, positions, length, filters, skip_gain, short_filter, in_proj, out_proj):
     tables = [jnp.asarray(table) for table in make_tables()]
-    vmem, smem, anywhere = (pl.BlockSpec(memory_space=m) for m in (pltpu.VMEM, pltpu.SMEM, pl.ANY))
+    inputs = [
+        length.reshape(1, 1),
+        positions.reshape(1, W),
+        events,
+        filters,
+        skip_gain,
+        short_filter,
+        in_proj,
+        out_proj,
+        *tables,
+    ]
     dma = lambda *shape: pltpu.SemaphoreType.DMA(shape)
+    held = [pltpu.VMEM((W, 2, 128) if i == 3 else x.shape, x.dtype) for i, x in enumerate(inputs)]
     return pl.pallas_call(
         functools.partial(kernel, n_batch),
         out_shape=jax.ShapeDtypeStruct((W, W), BF16),
-        in_specs=[smem] + [vmem] * 7 + [anywhere] * 5,
-        out_specs=vmem,
-        scratch_shapes=[pltpu.VMEM(table.shape, table.dtype) for table in tables]
+        in_specs=[pl.BlockSpec(memory_space=pl.ANY)] * INPUTS,
+        out_specs=pl.BlockSpec(memory_space=pltpu.VMEM),
+        scratch_shapes=held
         + [
             pltpu.VMEM((3, N, N, W), BF16),
-            pltpu.VMEM((8, W), jnp.int32),
+            pltpu.VMEM((1, W), jnp.int32),
             pltpu.VMEM((N, W), BF16),
             pltpu.VMEM((N, N, W), BF16),
             pltpu.VMEM((3, N, N, W), BF16),
-            pltpu.VMEM((N, 8, W), jnp.int32),
+            pltpu.VMEM((N, 1, W), jnp.int32),
             pltpu.VMEM((2, N, N, W), BF16),
             pltpu.VMEM((N, N, W), BF16),
             pltpu.VMEM((2, W, 2 * W), F32),
-            dma(5),
+            dma(INPUTS),
             dma(3, N),
             dma(3, N),
             dma(N),
@@ -380,19 +385,9 @@
             dma(N),
         ],
         compiler_params=pltpu.CompilerParams(
-            collective_id=0, has_side_effects=True, vmem_limit_bytes=48 * 1024 * 1024
+            collective_id=0, has_side_effects=True, vmem_limit_bytes=63 * 1024 * 1024
         ),
-    )(
-        length,
-        positions.reshape(1, W),
-        events,
-        filters.reshape(W, 2 * W),
-        skip_gain,
-        short_filter,
-        in_proj,
-        out_proj,
-        *tables,
-    )
+    )(*inputs)
 
 
 def solution(mesh):

time: 69.6 us -> 60 us (0.86)
  the two profiles are of different devices: /device:TPU:14 before, /device:TPU:4 now
where the time goes in v2:
time: 60 us; the launch traced here: 59.8 us
  Pallas kernels  57.6 us (96%)
  local copies, waits for them, and re-layouts  1.57 us (3%)
  between operations  0.66 us (1%)
    pallas_call x1, Pallas kernels, body(): pl.pallas_call(functools.partial(kernel, n_batch), out_shape=jax.ShapeDty...  57.6 us
    unnamed x1, local copies, waits for them, and re-layouts  1.57 us

profile of v2, /device:TPU:4, one launch (start us, length us, event | category | flops | bytes accessed | tf_op | source)
XLA Modules:
  0.0 59.8 jit_solution(5316548541982643649)
XLA Ops:
  0.7 57.6 %shard_map.127 = bf16[256,256]{1,0:T(8,128)(2,1)} custom-call(s32[1,1]{1,0:T(1,128)} %bitcast.2.refs_0_, s32[1,256]{1,0:T(1,128)} %bitcast.3, bf16[256,256]{1,0:T(8,128)(2,1)} %refs_2_.1, f32[256,2,256]{2,1,0:T(2,128)} %refs_3_.1, f32[2,256]{1,0:T(2,128)} %refs_4_.1, f32[3,768]{1,0:T(4,128)} %refs_5_.1, bf16[256,768]{1,0:T(8,128)(2,1)} %refs_6_.1, ...), custom_call_target="tpu_custom_call" | custom-call | tf_op jit(solution)/shard_map/pallas_call | solution.py:359
  58.2 1.6 %copy.16 = bf16[256,256]{1,0:T(8,128)(2,1)} copy(bf16[256,256]{1,0:T(8,128)(2,1)} %shard_map.127) | data formatting | bytes 262144

commit v3 on v2

v3 whole, which is shorter than its diff:
```python
import functools
import math

import jax
import jax.numpy as jnp
import ml_dtypes
import numpy as np
from jax import lax
from jax.experimental import pallas as pl
from jax.experimental.pallas import tpu as pltpu
from jax.sharding import PartitionSpec as P

N = 16
W = 256
POINTS = 2 * N * W
F32, BF16 = jnp.float32, jnp.bfloat16


def split(table):
    high = table.astype(ml_dtypes.bfloat16)
    low = (table - high.astype(np.float64)).astype(ml_dtypes.bfloat16)
    return high, low


@functools.cache
def make_tables():
    half = np.arange(N) + 0.5
    outer = 2 * np.pi * np.outer(half, np.arange(N)) / (2 * N)
    eye = np.eye(N)
    fwd_a = np.concatenate([np.kron(np.cos(outer), eye), np.kron(-np.sin(outer), eye)], 0)
    inv_a = np.concatenate([np.kron(np.cos(outer.T), eye), np.kron(-np.sin(outer.T), eye)], 1) * (2.0 / POINTS)
    inner = 2 * np.pi * (np.outer(np.arange(W), np.arange(W)) % W) / W
    cos, sin = np.cos(inner), np.sin(inner)
    fwd_b = np.block([[cos, -sin], [sin, cos]])
    inv_b = np.block([[cos, sin], [-sin, cos]])
    twist = 2 * np.pi * np.outer(half, np.arange(W)) / POINTS
    cat = lambda table, axis: np.concatenate([split(table)[i] for i in (0, 0, 1)], axis)
    return (
        cat(fwd_a, 1),
        cat(fwd_b, 0),
        cat(inv_b, 0),
        cat(inv_a, 1),
        np.stack([np.cos(twist), np.sin(twist)]).astype(np.float32),
    )


def parts(x, axis):
    high = x.astype(BF16)
    low = (x - high.astype(F32)).astype(BF16)
    return jnp.concatenate([high, low, high], axis=axis)


def dot(a, b, dims=((1,), (0,))):
    return lax.dot_general(a, b, (dims, ((), ())), preferred_element_type=F32)


INPUTS = 12


def kernel(n_batch, *refs):
    outside, (out, *inside), rest = refs[:INPUTS], refs[INPUTS : 2 * INPUTS + 1], refs[2 * INPUTS + 1 :]
    length, positions, events, filters, skip_gain, short_filter, in_proj, *tables = inside
    fwd_a, fwd_b, inv_b, inv_a, twist = tables
    (
        thirds,
        block_row,
        taps,
        gated,
        gate,
        passed,
        ids_row,
        recv_sig,
        recv_blk,
        recv_tap,
        spec,
        load_sem,
        sig_send,
        sig_recv,
        blk_send,
        blk_recv,
        tap_send,
        tap_recv,
        own_send,
        own_recv,
        twin_send,
        twin_recv,
        keep_sem,
        out_send,
        out_recv,
    ) = rest
    me = lax.axis_index("seq")
    lane = lax.axis_index("batch")
    column, core = lane // 2, lane % 2
    chips, sibling = n_batch // 2, column * 2 + 1 - core

    target = (me + column) % N
    loads = []
    for i, (src, dst) in enumerate(zip(outside, inside)):
        if i == 3:
            src = src.at[:, :, pl.ds(pl.multiple_of(target // 8 * 128, 128), 128)]
        loads.append(pltpu.make_async_copy(src, dst, load_sem.at[i]))
    for i in (1, 2, 6, 0, 3, 7, 11, 8, 5, 4, 9, 10):
        loads[i].start()

    barrier = pltpu.get_barrier_semaphore()

    def greet(k, carry):
        pl.semaphore_signal(barrier, inc=1, device_id={"seq": (me + k) % N})
        return carry

    def greet_plane(k, carry):
        pl.semaphore_signal(barrier, inc=1, device_id={"batch": (lane + 2 * k) % n_batch})
        return carry

    lax.fori_loop(1, N, greet, 0)
    lax.fori_loop(1, chips, greet_plane, 0)
    pl.semaphore_signal(barrier, inc=1, device_id={"batch": sibling})

    for i in (1, 0, 2, 6):
        loads[i].wait()
    pos = positions[...]
    order = lax.broadcasted_iota(jnp.int32, (W, W), 0) == pos % W
    one_hot = order.astype(BF16)
    kept = jnp.where(pos < length[...], one_hot, jnp.zeros_like(one_hot))
    ids = jnp.broadcast_to((pos // W).astype(BF16), (N, W))
    block_row[...] = dot(ids, one_hot, ((1,), (1,)))[0:1].astype(jnp.int32)
    ordered = dot(kept, events[...]).astype(BF16)

    def project(t):
        projected = dot(ordered, in_proj[:, t * W : (t + 1) * W])
        thirds[:, t] = projected.T.astype(BF16).reshape(N, N, W)

    project(0)
    loads[3].wait()
    rows16 = lax.broadcasted_iota(jnp.int32, (N, W), 0)
    lanes16 = lax.broadcasted_iota(jnp.int32, (N, W), 1)
    pick = (lanes16[:, :128] == rows16[:, :128] + target % 8 * N).astype(BF16)
    lags = jnp.where(core == 0, filters[:, 0, :], filters[:, 1, :]).astype(BF16)
    taps[...] = dot(pick, lags, ((1,), (1,))).astype(BF16)
    pl.semaphore_wait(barrier, N - 1 + chips)

    def tap_first():
        return pltpu.make_async_remote_copy(
            src_ref=taps,
            dst_ref=recv_tap.at[core, me],
            send_sem=own_send,
            recv_sem=own_recv,
            device_id={"seq": target},
        )

    slot = (me + N - column) % N

    def block_copy(k):
        peer = (me + k) % N
        return pltpu.make_async_remote_copy(
            src_ref=block_row,
            dst_ref=recv_blk.at[me],
            send_sem=blk_send.at[peer],
            recv_sem=blk_recv.at[me],
            device_id={"seq": peer},
        )

    def block_arrival(k):
        peer = (me + k) % N
        return pltpu.make_async_remote_copy(
            src_ref=block_row,
            dst_ref=recv_blk.at[peer],
            send_sem=blk_send.at[peer],
            recv_sem=blk_recv.at[peer],
            device_id={"seq": peer},
        )

    def sent(part):
        return pl.ds(0, 1) if part == 0 else pl.ds(1, 2)

    def third_copy(part, k):
        peer = (me + k) % N
        return pltpu.make_async_remote_copy(
            src_ref=thirds.at[peer, sent(part)],
            dst_ref=recv_sig.at[me, sent(part)],
            send_sem=sig_send.at[part, peer],
            recv_sem=sig_recv.at[part, me],
            device_id={"seq": peer},
        )

    def third_arrival(part, k):
        peer = (me + k) % N
        return pltpu.make_async_remote_copy(
            src_ref=thirds.at[peer, sent(part)],
            dst_ref=recv_sig.at[peer, sent(part)],
            send_sem=sig_send.at[part, peer],
            recv_sem=sig_recv.at[part, peer],
            device_id={"seq": peer},
        )

    def each(count, act):
        def step(k, carry):
            act(k)
            return carry

        lax.fori_loop(1, count, step, 0)

    @pl.when(column != 0)
    def _():
        tap_first().start()

    @pl.when(column == 0)
    def _():
        recv_tap[core, me] = taps[...]

    each(N, lambda k: block_copy(k).start())
    each(N, lambda k: third_copy(0, k).start())
    recv_blk[me] = block_row[...]
    project(1)
    project(2)
    recv_sig[me] = thirds[me]

    @pl.when(column != 0)
    def _():
        pltpu.make_async_remote_copy(
            src_ref=taps,
            dst_ref=recv_tap.at[core, slot],
            send_sem=own_send,
            recv_sem=own_recv,
            device_id={"seq": target},
        ).wait_recv()

    def tap_copy(k):
        peer = (column + k) % chips
        return pltpu.make_async_remote_copy(
            src_ref=recv_tap.at[core, slot],
            dst_ref=recv_tap.at[core, slot],
            send_sem=tap_send.at[peer],
            recv_sem=tap_recv.at[column],
            device_id={"batch": peer * 2 + core},
        )

    def tap_arrival(k):
        peer = (column + k) % chips
        there = recv_tap.at[core, (me + N - peer) % N]
        return pltpu.make_async_remote_copy(
            src_ref=there,
            dst_ref=there,
            send_sem=tap_send.at[peer],
            recv_sem=tap_recv.at[peer],
            device_id={"batch": peer * 2 + core},
        )

    def twin_copy(which):
        return pltpu.make_async_remote_copy(
            src_ref=recv_tap.at[which],
            dst_ref=recv_tap.at[which],
            send_sem=twin_send,
            recv_sem=twin_recv,
            device_id={"batch": sibling},
        )

    each(chips, lambda k: tap_copy(k).start())
    each(N, lambda k: third_copy(1, k).start())

    def column_of(row):
        return jnp.sum(jnp.where(lanes16 == rows16 + me * N, row, 0.0), axis=1, keepdims=True)[None]

    def rotate(re, im, sign):
        cos = twist[0][:, None, :]
        sin = twist[1][:, None, :] * sign
        re, im = re.reshape(N, N, W), im.reshape(N, N, W)
        return (re * cos + im * sin).reshape(W, W), (im * cos - re * sin).reshape(W, W)

    def forward(signal):
        mid = dot(fwd_a[...], parts(signal, 0))
        re, im = rotate(mid[:W], mid[W:], 1.0)
        return dot(parts(jnp.concatenate([re, im], axis=1), 1), fwd_b[...])

    def filtered(got, f):
        re, im = got[:, :W], got[:, W:]
        tap_re, tap_im = spec[f, :, :W], spec[f, :, W:]
        re, im = re * tap_re - im * tap_im, re * tap_im + im * tap_re
        mid = dot(parts(jnp.concatenate([re, im], axis=1), 1), inv_b[...])
        re, im = rotate(mid[:, :W], mid[:, W:], -1.0)
        return parts(jnp.concatenate([re, im], axis=0), 0)

    sub = lax.broadcasted_iota(jnp.int32, (W, W), 1)

    def short(t):
        rows = []
        for b in range(N):
            total = jnp.zeros((N, W), BF16)
            for s in range(N):
                total = jnp.where(ids_row[s] == b, recv_sig[s, t], total)
            rows.append(total)
        stream = jnp.concatenate(rows, axis=0).astype(F32)
        before = jnp.concatenate([jnp.zeros((N, W), F32), stream[:-N]], axis=0)
        one = pltpu.roll(jnp.where(sub == W - 1, before, stream), 1, 1)
        two = pltpu.roll(jnp.where(sub >= W - 2, before, stream), 2, 1)
        tap = [column_of(short_filter[i : i + 1, t * W : (t + 1) * W]) for i in range(3)]
        blocks = lambda x: x.reshape(N, N, W)
        return (tap[0] * blocks(stream) + tap[1] * blocks(one) + tap[2] * blocks(two)).reshape(W, W)

    each(chips, lambda k: tap_arrival(k).wait_recv())
    twin_copy(core).start()
    for i in (7, 11, 8, 5, 4):
        loads[i].wait()
    gain = [column_of(skip_gain[i : i + 1, :]) for i in range(2)]
    scaled = lambda g, x: (g * x.reshape(-1, N, W)).reshape(-1, W)

    each(N, lambda k: block_arrival(k).wait_recv())
    for s in range(N):
        ids_row[s] = jnp.broadcast_to(recv_blk[s].astype(F32), (N, W)).astype(BF16)
    each(N, lambda k: third_arrival(0, k).wait_recv())
    value = short(0)
    ahead = forward(value)
    twin_copy(1 - core).wait_recv()
    spec[0] = forward(recv_tap[0].reshape(W, W).astype(F32))
    for i in (9, 10):
        loads[i].wait()
    first = dot(inv_a[...], filtered(ahead, 0)) + scaled(gain[0], value)
    spec[1] = forward(recv_tap[1].reshape(W, W).astype(F32))
    each(N, lambda k: third_arrival(1, k).wait_recv())
    first = short(1) * first
    gate[...] = short(2)
    passed[...] = scaled(gain[1], first)
    ahead = filtered(forward(first), 1)
    def out_copy(k):
        peer = (me + k) % N
        return pltpu.make_async_remote_copy(
            src_ref=gated.at[peer],
            dst_ref=out.at[me],
            send_sem=out_send.at[peer],
            recv_sem=out_recv.at[me],
            device_id={"seq": peer},
        )

    def out_arrival(k):
        peer = (me + k) % N
        return pltpu.make_async_remote_copy(
            src_ref=gated.at[peer],
            dst_ref=out.at[peer],
            send_sem=out_send.at[peer],
            recv_sem=out_recv.at[peer],
            device_id={"seq": peer},
        )

    for g in range(4):
        group = (me // 4 + g) % 4
        at = pl.ds(pl.multiple_of(group * 64, 64), 64)
        rows = gate[at, :] * (dot(inv_a[at, :], ahead) + passed[at, :])
        gated[pl.ds(group * 4, 4)] = rows.astype(BF16).reshape(4, N, W)
        for i in range(4):
            peer = group * 4 + i

            @pl.when(peer != me)
            def _():
                out_copy((peer + N - me) % N).start()

    own = pltpu.make_async_copy(gated.at[me], out.at[me], keep_sem)
    own.start()

    @pl.when(column != 0)
    def _():
        tap_first().wait_send()

    each(N, lambda k: block_copy(k).wait_send())
    for part in range(2):
        each(N, lambda k: third_copy(part, k).wait_send())
    each(chips, lambda k: tap_copy(k).wait_send())
    twin_copy(core).wait_send()
    each(N, lambda k: out_copy(k).wait_send())
    each(N, lambda k: out_arrival(k).wait_recv())
    own.wait()


def body(n_batch, events, positions, length, filters, skip_gain, short_filter, in_proj, out_proj):
    tables = [jnp.asarray(table) for table in make_tables()]
    inputs = [
        length.reshape(1, 1),
        positions.reshape(1, W),
        events,
        filters,
        skip_gain,
        short_filter,
        in_proj,
        *tables,
    ]
    dma = lambda *shape: pltpu.SemaphoreType.DMA(shape)
    held = [pltpu.VMEM((W, 2, 128) if i == 3 else x.shape, x.dtype) for i, x in enumerate(inputs)]
    gated = pl.pallas_call(
        functools.partial(kernel, n_batch),
        out_shape=jax.ShapeDtypeStruct((N, N, W), BF16),
        in_specs=[pl.BlockSpec(memory_space=pl.ANY)] * INPUTS,
        out_specs=pl.BlockSpec(memory_space=pl.ANY),
        scratch_shapes=held
        + [
            pltpu.VMEM((N, 3, N, W), BF16),
            pltpu.VMEM((1, W), jnp.int32),
            pltpu.VMEM((N, W), BF16),
            pltpu.VMEM((N, N, W), BF16),
            pltpu.VMEM((W, W), F32),
            pltpu.VMEM((W, W), F32),
            pltpu.VMEM((N, N, W), BF16),
            pltpu.VMEM((N, 3, N, W), BF16),
            pltpu.VMEM((N, 1, W), jnp.int32),
            pltpu.VMEM((2, N, N, W), BF16),
            pltpu.VMEM((2, W, 2 * W), F32),
            dma(INPUTS),
            dma(2, N),
            dma(2, N),
            dma(N),
            dma(N),
            dma(n_batch // 2),
            dma(n_batch // 2),
            pltpu.SemaphoreType.DMA,
            pltpu.SemaphoreType.DMA,
            pltpu.SemaphoreType.DMA,
            pltpu.SemaphoreType.DMA,
            pltpu.SemaphoreType.DMA,
            dma(N),
            dma(N),
        ],
        compiler_params=pltpu.CompilerParams(
            collective_id=0, has_side_effects=True, vmem_limit_bytes=63 * 1024 * 1024
        ),
    )(*inputs)
    return dot(gated.reshape(W, W), out_proj, ((0,), (0,))).astype(BF16)


def solution(mesh):
    return jax.shard_map(
        functools.partial(body, mesh.shape["batch"]),
        mesh=mesh,
        in_specs=(
            P(("batch", "seq"), None),
            P(("batch", "seq")),
            P("batch"),
            P("seq", None, None),
            P(),
            P(),
            P(),
            P(),
        ),
        out_specs=P(("batch", "seq"), None),
        check_vma=False,
    )
```

time: 60 us -> 56.1 us (0.935)
  the two profiles are of different devices: /device:TPU:4 before, /device:TPU:12 now
where the time goes in v3:
time: 56.1 us; the launch traced here: 56 us
  Pallas kernels  53.5 us (95%)
  matrix products  1.79 us (3%)
  between operations  0.7 us (1%)
    pallas_call x1, Pallas kernels, body(): pl.pallas_call(functools.partial(kernel, n_batch), out_shape=jax.ShapeDty...  53.5 us
    dot_general x1, matrix products, dot(): return lax.dot_general(a, b, (dims, ((), ())), preferred_element_type=F32)  1.79 us

profile of v3, /device:TPU:12, one launch (start us, length us, event | category | flops | bytes accessed | tf_op | source)
XLA Modules:
  0.0 56.0 jit_solution(8986237222788099952)
XLA Ops:
  0.0 0.0 copy-start
  0.7 53.5 %shard_map.127 = bf16[16,16,256]{2,1,0:T(8,128)(2,1)} custom-call(s32[1,1]{1,0:T(1,128)} %bitcast.5.refs_0_, s32[1,256]{1,0:T(1,128)} %bitcast.7, bf16[256,256]{1,0:T(8,128)(2,1)} %refs_2_.1, f32[256,2,256]{2,1,0:T(2,128)} %refs_3_.1, f32[2,256]{1,0:T(2,128)} %refs_4_.1, f32[3,768]{1,0:T(4,128)} %refs_5_.1, bf16[256,768]{1,0:T(8,128)(2,1)} %refs_6_.1, ...), custom_call_target="tpu_custom_call" | custom-call | tf_op jit(solution)/shard_map/pallas_call | solution.py:387
  54.2 0.0 copy-done
  54.2 1.8 %convolution_convert_fusion = bf16[256,256]{1,0:T(8,128)(2,1)} fusion(bf16[256,256]{1,0:T(8,128)(2,1)} %bitcast.6, bf16[256,256]{1,0:T(8,128)(2,1)S(1)} %copy-done), kind=kOutput, calls=%fused_computation | convolution fusion | flops 33619968 | bytes 393216 | tf_op jit(solution)/shard_map/dot_general | solution.py:54
Async XLA Ops:
  0.0 54.2 %copy-start = (bf16[256,256]{1,0:T(8,128)(2,1)S(1)}, bf16[256,256]{1,0:T(8,128)(2,1)}, u32[]{:S(2)}) copy-start(bf16[256,256]{1,0:T(8,128)(2,1)} %param.20) | copy-start | bytes 393220

commit v4 on v3

--- a/solution.py
+++ b/solution.py
@@ -11,6 +11,7 @@
 from jax.sharding import PartitionSpec as P
 
 N = 16
+FAR = (8, 7, 9, 6, 10, 5, 11, 4, 12, 3, 13, 2, 14, 1, 15)
 W = 256
 POINTS = 2 * N * W
 F32, BF16 = jnp.float32, jnp.bfloat16
@@ -82,8 +83,6 @@
         tap_recv,
         own_send,
         own_recv,
-        twin_send,
-        twin_recv,
         keep_sem,
         out_send,
         out_recv,
@@ -91,30 +90,23 @@
     me = lax.axis_index("seq")
     lane = lax.axis_index("batch")
     column, core = lane // 2, lane % 2
-    chips, sibling = n_batch // 2, column * 2 + 1 - core
-
+    chips = n_batch // 2
     target = (me + column) % N
+
+    barrier = pltpu.get_barrier_semaphore()
+    for k in FAR:
+        pl.semaphore_signal(barrier, inc=1, device_id={"seq": (me + k) % N})
     loads = []
     for i, (src, dst) in enumerate(zip(outside, inside)):
         if i == 3:
             src = src.at[:, :, pl.ds(pl.multiple_of(target // 8 * 128, 128), 128)]
         loads.append(pltpu.make_async_copy(src, dst, load_sem.at[i]))
-    for i in (1, 2, 6, 0, 3, 7, 11, 8, 5, 4, 9, 10):
+    for i in (1, 2, 6, 0, 3):
         loads[i].start()
-
-    barrier = pltpu.get_barrier_semaphore()
-
-    def greet(k, carry):
-        pl.semaphore_signal(barrier, inc=1, device_id={"seq": (me + k) % N})
-        return carry
-
-    def greet_plane(k, carry):
+    for k in range(1, chips):
         pl.semaphore_signal(barrier, inc=1, device_id={"batch": (lane + 2 * k) % n_batch})
-        return carry
-
-    lax.fori_loop(1, N, greet, 0)
-    lax.fori_loop(1, chips, greet_plane, 0)
-    pl.semaphore_signal(barrier, inc=1, device_id={"batch": sibling})
+    for i in (7, 11, 8, 5, 4, 9, 10):
+        loads[i].start()
 
     for i in (1, 0, 2, 6):
         loads[i].wait()
@@ -131,18 +123,20 @@
         thirds[:, t] = projected.T.astype(BF16).reshape(N, N, W)
 
     project(0)
+    project(1)
+    project(2)
     loads[3].wait()
     rows16 = lax.broadcasted_iota(jnp.int32, (N, W), 0)
     lanes16 = lax.broadcasted_iota(jnp.int32, (N, W), 1)
     pick = (lanes16[:, :128] == rows16[:, :128] + target % 8 * N).astype(BF16)
-    lags = jnp.where(core == 0, filters[:, 0, :], filters[:, 1, :]).astype(BF16)
-    taps[...] = dot(pick, lags, ((1,), (1,))).astype(BF16)
-    pl.semaphore_wait(barrier, N - 1 + chips)
+    for f in range(2):
+        taps[f] = dot(pick, filters[:, f, :].astype(BF16), ((1,), (1,))).astype(BF16)
+    pl.semaphore_wait(barrier, N - 1 + chips - 1)
 
     def tap_first():
         return pltpu.make_async_remote_copy(
             src_ref=taps,
-            dst_ref=recv_tap.at[core, me],
+            dst_ref=recv_tap.at[me],
             send_sem=own_send,
             recv_sem=own_recv,
             device_id={"seq": target},
@@ -170,14 +164,11 @@
             device_id={"seq": peer},
         )
 
-    def sent(part):
-        return pl.ds(0, 1) if part == 0 else pl.ds(1, 2)
-
     def third_copy(part, k):
         peer = (me + k) % N
         return pltpu.make_async_remote_copy(
-            src_ref=thirds.at[peer, sent(part)],
-            dst_ref=recv_sig.at[me, sent(part)],
+            src_ref=thirds.at[peer, part],
+            dst_ref=recv_sig.at[me, part],
             send_sem=sig_send.at[part, peer],
             recv_sem=sig_recv.at[part, me],
             device_id={"seq": peer},
@@ -186,8 +177,8 @@
     def third_arrival(part, k):
         peer = (me + k) % N
         return pltpu.make_async_remote_copy(
-            src_ref=thirds.at[peer, sent(part)],
-            dst_ref=recv_sig.at[peer, sent(part)],
+            src_ref=thirds.at[peer, part],
+            dst_ref=recv_sig.at[peer, part],
             send_sem=sig_send.at[part, peer],
             recv_sem=sig_recv.at[part, peer],
             device_id={"seq": peer},
@@ -206,20 +197,22 @@
 
     @pl.when(column == 0)
     def _():
-        recv_tap[core, me] = taps[...]
-
-    each(N, lambda k: block_copy(k).start())
-    each(N, lambda k: third_copy(0, k).start())
+        recv_tap[me] = taps[...]
+
+    for k in FAR:
+        block_copy(k).start()
+        third_copy(0, k).start()
+    for part in (1, 2):
+        for k in FAR:
+            third_copy(part, k).start()
     recv_blk[me] = block_row[...]
-    project(1)
-    project(2)
     recv_sig[me] = thirds[me]
 
     @pl.when(column != 0)
     def _():
         pltpu.make_async_remote_copy(
             src_ref=taps,
-            dst_ref=recv_tap.at[core, slot],
+            dst_ref=recv_tap.at[slot],
             send_sem=own_send,
             recv_sem=own_recv,
             device_id={"seq": target},
@@ -228,8 +221,8 @@
     def tap_copy(k):
         peer = (column + k) % chips
         return pltpu.make_async_remote_copy(
-            src_ref=recv_tap.at[core, slot],
-            dst_ref=recv_tap.at[core, slot],
+            src_ref=recv_tap.at[slot],
+            dst_ref=recv_tap.at[slot],
             send_sem=tap_send.at[peer],
             recv_sem=tap_recv.at[column],
             device_id={"batch": peer * 2 + core},
@@ -237,7 +230,7 @@
 
     def tap_arrival(k):
         peer = (column + k) % chips
-        there = recv_tap.at[core, (me + N - peer) % N]
+        there = recv_tap.at[(me + N - peer) % N]
         return pltpu.make_async_remote_copy(
             src_ref=there,
             dst_ref=there,
@@ -246,17 +239,8 @@
             device_id={"batch": peer * 2 + core},
         )
 
-    def twin_copy(which):
-        return pltpu.make_async_remote_copy(
-            src_ref=recv_tap.at[which],
-            dst_ref=recv_tap.at[which],
-            send_sem=twin_send,
-            recv_sem=twin_recv,
-            device_id={"batch": sibling},
-        )
-
-    each(chips, lambda k: tap_copy(k).start())
-    each(N, lambda k: third_copy(1, k).start())
+    for k in range(1, chips):
+        tap_copy(k).start()
 
     def column_of(row):
         return jnp.sum(jnp.where(lanes16 == rows16 + me * N, row, 0.0), axis=1, keepdims=True)[None]
@@ -297,12 +281,11 @@
         blocks = lambda x: x.reshape(N, N, W)
         return (tap[0] * blocks(stream) + tap[1] * blocks(one) + tap[2] * blocks(two)).reshape(W, W)
 
-    each(chips, lambda k: tap_arrival(k).wait_recv())
-    twin_copy(core).start()
-    for i in (7, 11, 8, 5, 4):
+    for i in (7, 11, 8, 5, 4, 9, 10):
         loads[i].wait()
     gain = [column_of(skip_gain[i : i + 1, :]) for i in range(2)]
     scaled = lambda g, x: (g * x.reshape(-1, N, W)).reshape(-1, W)
+    spectrum = lambda f: forward(recv_tap[:, f].reshape(W, W).astype(F32))
 
     each(N, lambda k: block_arrival(k).wait_recv())
     for s in range(N):
@@ -310,17 +293,17 @@
     each(N, lambda k: third_arrival(0, k).wait_recv())
     value = short(0)
     ahead = forward(value)
-    twin_copy(1 - core).wait_recv()
-    spec[0] = forward(recv_tap[0].reshape(W, W).astype(F32))
-    for i in (9, 10):
-        loads[i].wait()
-    first = dot(inv_a[...], filtered(ahead, 0)) + scaled(gain[0], value)
-    spec[1] = forward(recv_tap[1].reshape(W, W).astype(F32))
     each(N, lambda k: third_arrival(1, k).wait_recv())
-    first = short(1) * first
+    gate[...] = short(1)
+    each(chips, lambda k: tap_arrival(k).wait_recv())
+    spec[0] = spectrum(0)
+    first = gate[...] * (dot(inv_a[...], filtered(ahead, 0)) + scaled(gain[0], value))
+    passed[...] = scaled(gain[1], first)
+    spec[1] = spectrum(1)
+    ahead = filtered(forward(first), 1)
+    each(N, lambda k: third_arrival(2, k).wait_recv())
     gate[...] = short(2)
-    passed[...] = scaled(gain[1], first)
-    ahead = filtered(forward(first), 1)
+
     def out_copy(k):
         peer = (me + k) % N
         return pltpu.make_async_remote_copy(
@@ -341,7 +324,7 @@
             device_id={"seq": peer},
         )
 
-    for g in range(4):
+    for g in (2, 1, 3, 0):
         group = (me // 4 + g) % 4
         at = pl.ds(pl.multiple_of(group * 64, 64), 64)
         rows = gate[at, :] * (dot(inv_a[at, :], ahead) + passed[at, :])
@@ -361,10 +344,9 @@
         tap_first().wait_send()
 
     each(N, lambda k: block_copy(k).wait_send())
-    for part in range(2):
+    for part in range(3):
         each(N, lambda k: third_copy(part, k).wait_send())
     each(chips, lambda k: tap_copy(k).wait_send())
-    twin_copy(core).wait_send()
     each(N, lambda k: out_copy(k).wait_send())
     each(N, lambda k: out_arrival(k).wait_recv())
     own.wait()
@@ -393,24 +375,22 @@
         + [
             pltpu.VMEM((N, 3, N, W), BF16),
             pltpu.VMEM((1, W), jnp.int32),
-            pltpu.VMEM((N, W), BF16),
+            pltpu.VMEM((2, N, W), BF16),
             pltpu.VMEM((N, N, W), BF16),
             pltpu.VMEM((W, W), F32),
             pltpu.VMEM((W, W), F32),
             pltpu.VMEM((N, N, W), BF16),
             pltpu.VMEM((N, 3, N, W), BF16),
             pltpu.VMEM((N, 1, W), jnp.int32),
-            pltpu.VMEM((2, N, N, W), BF16),
+            pltpu.VMEM((N, 2, N, W), BF16),
             pltpu.VMEM((2, W, 2 * W), F32),
             dma(INPUTS),
-            dma(2, N),
-            dma(2, N),
+            dma(3, N),
+            dma(3, N),
             dma(N),
             dma(N),
             dma(n_batch // 2),
             dma(n_batch // 2),
-            pltpu.SemaphoreType.DMA,
-            pltpu.SemaphoreType.DMA,
             pltpu.SemaphoreType.DMA,
             pltpu.SemaphoreType.DMA,
             pltpu.SemaphoreType.DMA,

time: 56.1 us -> 50.2 us (0.89)
  the two profiles are of different devices: /device:TPU:12 before, /device:TPU:14 now
where the time goes in v4:
time: 50.2 us; the launch traced here: 50.1 us
  Pallas kernels  47.6 us (95%)
  matrix products  1.79 us (4%)
  between operations  0.7 us (1%)
    pallas_call x1, Pallas kernels, body(): pl.pallas_call(functools.partial(kernel, n_batch), out_shape=jax.ShapeDty...  47.6 us
    dot_general x1, matrix products, dot(): return lax.dot_general(a, b, (dims, ((), ())), preferred_element_type=F32)  1.79 us

profile of v4, /device:TPU:14, one launch (start us, length us, event | category | flops | bytes accessed | tf_op | source)
XLA Modules:
  0.0 50.1 jit_solution(2038791085163644834)
XLA Ops:
  0.0 0.0 copy-start
  0.7 47.6 %shard_map.127 = bf16[16,16,256]{2,1,0:T(8,128)(2,1)} custom-call(s32[1,1]{1,0:T(1,128)} %bitcast.5.refs_0_, s32[1,256]{1,0:T(1,128)} %bitcast.7, bf16[256,256]{1,0:T(8,128)(2,1)} %refs_2_.1, f32[256,2,256]{2,1,0:T(2,128)} %refs_3_.1, f32[2,256]{1,0:T(2,128)} %refs_4_.1, f32[3,768]{1,0:T(4,128)} %refs_5_.1, bf16[256,768]{1,0:T(8,128)(2,1)} %refs_6_.1, ...), custom_call_target="tpu_custom_call" | custom-call | tf_op jit(solution)/shard_map/pallas_call | solution.py:369
  48.3 0.0 copy-done
  48.3 1.8 %convolution_convert_fusion = bf16[256,256]{1,0:T(8,128)(2,1)} fusion(bf16[256,256]{1,0:T(8,128)(2,1)} %bitcast.6, bf16[256,256]{1,0:T(8,128)(2,1)S(1)} %copy-done), kind=kOutput, calls=%fused_computation | convolution fusion | flops 33619968 | bytes 393216 | tf_op jit(solution)/shard_map/dot_general | solution.py:55
Async XLA Ops:
  0.0 48.3 %copy-start = (bf16[256,256]{1,0:T(8,128)(2,1)S(1)}, bf16[256,256]{1,0:T(8,128)(2,1)}, u32[]{:S(2)}) copy-start(bf16[256,256]{1,0:T(8,128)(2,1)} %param.20) | copy-start | bytes 393220

commit v5 on v4

--- a/solution.py
+++ b/solution.py
@@ -35,11 +35,11 @@
     fwd_b = np.block([[cos, -sin], [sin, cos]])
     inv_b = np.block([[cos, sin], [-sin, cos]])
     twist = 2 * np.pi * np.outer(half, np.arange(W)) / POINTS
-    cat = lambda table, axis: np.concatenate([split(table)[i] for i in (0, 0, 1)], axis)
+    cat = lambda table, axis, order=(0, 0, 1): np.concatenate([split(table)[i] for i in order], axis)
     return (
         cat(fwd_a, 1),
-        cat(fwd_b, 0),
-        cat(inv_b, 0),
+        cat(fwd_b, 0, (0, 1)),
+        cat(inv_b, 0, (0, 1)),
         cat(inv_a, 1),
         np.stack([np.cos(twist), np.sin(twist)]).astype(np.float32),
     )
@@ -202,9 +202,8 @@
     for k in FAR:
         block_copy(k).start()
         third_copy(0, k).start()
-    for part in (1, 2):
-        for k in FAR:
-            third_copy(part, k).start()
+    for k in FAR:
+        third_copy(1, k).start()
     recv_blk[me] = block_row[...]
     recv_sig[me] = thirds[me]
 
@@ -241,6 +240,8 @@
 
     for k in range(1, chips):
         tap_copy(k).start()
+    for k in FAR:
+        third_copy(2, k).start()
 
     def column_of(row):
         return jnp.sum(jnp.where(lanes16 == rows16 + me * N, row, 0.0), axis=1, keepdims=True)[None]
@@ -251,16 +252,23 @@
         re, im = re.reshape(N, N, W), im.reshape(N, N, W)
         return (re * cos + im * sin).reshape(W, W), (im * cos - re * sin).reshape(W, W)
 
+    def inner(re, im, table):
+        x = jnp.concatenate([re, im], axis=1).astype(BF16)
+        return dot(jnp.concatenate([x, x], axis=1), table[...])
+
     def forward(signal):
-        mid = dot(fwd_a[...], parts(signal, 0))
+        if signal.dtype == BF16:
+            mid = dot(fwd_a[:, W:], jnp.concatenate([signal, signal], axis=0))
+        else:
+            mid = dot(fwd_a[...], parts(signal, 0))
         re, im = rotate(mid[:W], mid[W:], 1.0)
-        return dot(parts(jnp.concatenate([re, im], axis=1), 1), fwd_b[...])
+        return inner(re, im, fwd_b)
 
     def filtered(got, f):
         re, im = got[:, :W], got[:, W:]
         tap_re, tap_im = spec[f, :, :W], spec[f, :, W:]
         re, im = re * tap_re - im * tap_im, re * tap_im + im * tap_re
-        mid = dot(parts(jnp.concatenate([re, im], axis=1), 1), inv_b[...])
+        mid = inner(re, im, inv_b)
         re, im = rotate(mid[:, :W], mid[:, W:], -1.0)
         return parts(jnp.concatenate([re, im], axis=0), 0)
 
@@ -285,23 +293,28 @@
         loads[i].wait()
     gain = [column_of(skip_gain[i : i + 1, :]) for i in range(2)]
     scaled = lambda g, x: (g * x.reshape(-1, N, W)).reshape(-1, W)
-    spectrum = lambda f: forward(recv_tap[:, f].reshape(W, W).astype(F32))
-
-    each(N, lambda k: block_arrival(k).wait_recv())
+    spectrum = lambda f: forward(recv_tap[:, f].reshape(W, W))
+
+    for k in FAR[::-1]:
+        block_arrival(k).wait_recv()
     for s in range(N):
         ids_row[s] = jnp.broadcast_to(recv_blk[s].astype(F32), (N, W)).astype(BF16)
-    each(N, lambda k: third_arrival(0, k).wait_recv())
+    for k in FAR[::-1]:
+        third_arrival(0, k).wait_recv()
     value = short(0)
     ahead = forward(value)
-    each(N, lambda k: third_arrival(1, k).wait_recv())
+    for k in FAR[::-1]:
+        third_arrival(1, k).wait_recv()
     gate[...] = short(1)
-    each(chips, lambda k: tap_arrival(k).wait_recv())
+    for k in range(1, chips):
+        tap_arrival(k).wait_recv()
     spec[0] = spectrum(0)
     first = gate[...] * (dot(inv_a[...], filtered(ahead, 0)) + scaled(gain[0], value))
     passed[...] = scaled(gain[1], first)
     spec[1] = spectrum(1)
     ahead = filtered(forward(first), 1)
-    each(N, lambda k: third_arrival(2, k).wait_recv())
+    for k in FAR[::-1]:
+        third_arrival(2, k).wait_recv()
     gate[...] = short(2)
 
     def out_copy(k):
@@ -348,7 +361,8 @@
         each(N, lambda k: third_copy(part, k).wait_send())
     each(chips, lambda k: tap_copy(k).wait_send())
     each(N, lambda k: out_copy(k).wait_send())
-    each(N, lambda k: out_arrival(k).wait_recv())
+    for k in FAR[::-1]:
+        out_arrival(k).wait_recv()
     own.wait()
 
 

time: 50.2 us -> 49.7 us (0.990)
    pallas_call x1, Pallas kernels: 47.6 us -> 47.1 us  [body(): pl.pallas_call(functools.partial(kernel, n_batch), out_shape=jax.ShapeDty...]
where the time goes in v5:
time: 49.7 us; the launch traced here: 49.6 us
  Pallas kernels  47.1 us (95%)
  matrix products  1.79 us (4%)
  between operations  0.7 us (1%)
    pallas_call x1, Pallas kernels, body(): pl.pallas_call(functools.partial(kernel, n_batch), out_shape=jax.ShapeDty...  47.1 us
    dot_general x1, matrix products, dot(): return lax.dot_general(a, b, (dims, ((), ())), preferred_element_type=F32)  1.79 us

profile of v5, /device:TPU:14, one launch (start us, length us, event | category | flops | bytes accessed | tf_op | source)
XLA Modules:
  0.0 49.6 jit_solution(1750745319714223883)
XLA Ops:
  0.0 0.0 copy-start
  0.7 47.1 %shard_map.127 = bf16[16,16,256]{2,1,0:T(8,128)(2,1)} custom-call(s32[1,1]{1,0:T(1,128)} %bitcast.5.refs_0_, s32[1,256]{1,0:T(1,128)} %bitcast.7, bf16[256,256]{1,0:T(8,128)(2,1)} %refs_2_.1, f32[256,2,256]{2,1,0:T(2,128)} %refs_3_.1, f32[2,256]{1,0:T(2,128)} %refs_4_.1, f32[3,768]{1,0:T(4,128)} %refs_5_.1, bf16[256,768]{1,0:T(8,128)(2,1)} %refs_6_.1, ...), custom_call_target="tpu_custom_call" | custom-call | tf_op jit(solution)/shard_map/pallas_call | solution.py:383
  47.8 0.0 copy-done
  47.8 1.8 %convolution_convert_fusion = bf16[256,256]{1,0:T(8,128)(2,1)} fusion(bf16[256,256]{1,0:T(8,128)(2,1)} %bitcast.6, bf16[256,256]{1,0:T(8,128)(2,1)S(1)} %copy-done), kind=kOutput, calls=%fused_computation | convolution fusion | flops 33619968 | bytes 393216 | tf_op jit(solution)/shard_map/dot_general | solution.py:55
Async XLA Ops:
  0.0 47.8 %copy-start = (bf16[256,256]{1,0:T(8,128)(2,1)S(1)}, bf16[256,256]{1,0:T(8,128)(2,1)}, u32[]{:S(2)}) copy-start(bf16[256,256]{1,0:T(8,128)(2,1)} %param.20) | copy-start | bytes 393220

commit v6 on v5

--- a/solution.py
+++ b/solution.py
@@ -91,7 +91,8 @@
     lane = lax.axis_index("batch")
     column, core = lane // 2, lane % 2
     chips = n_batch // 2
-    target = (me + column) % N
+    shift = (column + N // 2 * core) % N
+    target = (me + shift) % N
 
     barrier = pltpu.get_barrier_semaphore()
     for k in FAR:
@@ -123,8 +124,6 @@
         thirds[:, t] = projected.T.astype(BF16).reshape(N, N, W)
 
     project(0)
-    project(1)
-    project(2)
     loads[3].wait()
     rows16 = lax.broadcasted_iota(jnp.int32, (N, W), 0)
     lanes16 = lax.broadcasted_iota(jnp.int32, (N, W), 1)
@@ -142,7 +141,7 @@
             device_id={"seq": target},
         )
 
-    slot = (me + N - column) % N
+    slot = (me + N - shift) % N
 
     def block_copy(k):
         peer = (me + k) % N
@@ -191,23 +190,25 @@
 
         lax.fori_loop(1, count, step, 0)
 
-    @pl.when(column != 0)
+    @pl.when(shift != 0)
     def _():
         tap_first().start()
 
-    @pl.when(column == 0)
+    @pl.when(shift == 0)
     def _():
         recv_tap[me] = taps[...]
 
     for k in FAR:
         block_copy(k).start()
         third_copy(0, k).start()
+    project(1)
     for k in FAR:
         third_copy(1, k).start()
+    project(2)
     recv_blk[me] = block_row[...]
     recv_sig[me] = thirds[me]
 
-    @pl.when(column != 0)
+    @pl.when(shift != 0)
     def _():
         pltpu.make_async_remote_copy(
             src_ref=taps,
@@ -229,7 +230,7 @@
 
     def tap_arrival(k):
         peer = (column + k) % chips
-        there = recv_tap.at[(me + N - peer) % N]
+        there = recv_tap.at[(me + N - (peer + N // 2 * core) % N) % N]
         return pltpu.make_async_remote_copy(
             src_ref=there,
             dst_ref=there,
@@ -337,22 +338,13 @@
             device_id={"seq": peer},
         )
 
-    for g in (2, 1, 3, 0):
-        group = (me // 4 + g) % 4
-        at = pl.ds(pl.multiple_of(group * 64, 64), 64)
-        rows = gate[at, :] * (dot(inv_a[at, :], ahead) + passed[at, :])
-        gated[pl.ds(group * 4, 4)] = rows.astype(BF16).reshape(4, N, W)
-        for i in range(4):
-            peer = group * 4 + i
-
-            @pl.when(peer != me)
-            def _():
-                out_copy((peer + N - me) % N).start()
-
+    gated[...] = (gate[...] * (dot(inv_a[...], ahead) + passed[...])).astype(BF16).reshape(N, N, W)
+    for k in FAR:
+        out_copy(k).start()
     own = pltpu.make_async_copy(gated.at[me], out.at[me], keep_sem)
     own.start()
 
-    @pl.when(column != 0)
+    @pl.when(shift != 0)
     def _():
         tap_first().wait_send()
 

time: 49.7 us -> 49.3 us (level)
  the two profiles are of different devices: /device:TPU:14 before, /device:TPU:30 now
where the time goes in v6:
time: 49.3 us; the launch traced here: 49.1 us
  Pallas kernels  46.6 us (95%)
  matrix products  1.79 us (4%)
  between operations  0.7 us (1%)
    pallas_call x1, Pallas kernels, body(): pl.pallas_call(functools.partial(kernel, n_batch), out_shape=jax.ShapeDty...  46.6 us
    dot_general x1, matrix products, dot(): return lax.dot_general(a, b, (dims, ((), ())), preferred_element_type=F32)  1.79 us

profile of v6, /device:TPU:30, one launch (start us, length us, event | category | flops | bytes accessed | tf_op | source)
XLA Modules:
  0.0 49.1 jit_solution(12959440369021026854)
XLA Ops:
  0.0 0.0 copy-start
  0.7 46.6 %shard_map.127 = bf16[16,16,256]{2,1,0:T(8,128)(2,1)} custom-call(s32[1,1]{1,0:T(1,128)} %bitcast.5.refs_0_, s32[1,256]{1,0:T(1,128)} %bitcast.7, bf16[256,256]{1,0:T(8,128)(2,1)} %refs_2_.1, f32[256,2,256]{2,1,0:T(2,128)} %refs_3_.1, f32[2,256]{1,0:T(2,128)} %refs_4_.1, f32[3,768]{1,0:T(4,128)} %refs_5_.1, bf16[256,768]{1,0:T(8,128)(2,1)} %refs_6_.1, ...), custom_call_target="tpu_custom_call" | custom-call | tf_op jit(solution)/shard_map/pallas_call | solution.py:375
  47.3 0.0 copy-done
  47.4 1.8 %convolution_convert_fusion = bf16[256,256]{1,0:T(8,128)(2,1)} fusion(bf16[256,256]{1,0:T(8,128)(2,1)} %bitcast.6, bf16[256,256]{1,0:T(8,128)(2,1)S(1)} %copy-done), kind=kOutput, calls=%fused_computation | convolution fusion | flops 33619968 | bytes 393216 | tf_op jit(solution)/shard_map/dot_general | solution.py:55
Async XLA Ops:
  0.0 47.3 %copy-start = (bf16[256,256]{1,0:T(8,128)(2,1)S(1)}, bf16[256,256]{1,0:T(8,128)(2,1)}, u32[]{:S(2)}) copy-start(bf16[256,256]{1,0:T(8,128)(2,1)} %param.20) | copy-start | bytes 393220

commit v7 on v6

--- a/solution.py
+++ b/solution.py
@@ -59,7 +59,7 @@
 
 
 def kernel(n_batch, *refs):
-    outside, (out, *inside), rest = refs[:INPUTS], refs[INPUTS : 2 * INPUTS + 1], refs[2 * INPUTS + 1 :]
+    outside, (out, side, *inside), rest = refs[:INPUTS], refs[INPUTS : 2 * INPUTS + 2], refs[2 * INPUTS + 2 :]
     length, positions, events, filters, skip_gain, short_filter, in_proj, *tables = inside
     fwd_a, fwd_b, inv_b, inv_a, twist = tables
     (
@@ -70,6 +70,10 @@
         gate,
         passed,
         ids_row,
+        sent_rows,
+        recv_rows,
+        tail_rows,
+        halo,
         recv_sig,
         recv_blk,
         recv_tap,
@@ -84,6 +88,9 @@
         own_send,
         own_recv,
         keep_sem,
+        side_sem,
+        halo_send,
+        halo_recv,
         out_send,
         out_recv,
     ) = rest
@@ -204,9 +211,42 @@
     project(1)
     for k in FAR:
         third_copy(1, k).start()
-    project(2)
+    by_block = lax.broadcasted_iota(jnp.int32, (W, W), 0) == pos // W * N + pos % N
+    by_block = jnp.where(by_block & (pos < length[...]), 1.0, 0.0).astype(BF16)
+    rows = dot(by_block, events[...]).astype(BF16)
+    sent_rows[...] = dot(rows, in_proj[:, 2 * W :]).astype(BF16).reshape(N, N, W)
+    recv_rows[me] = sent_rows[me]
     recv_blk[me] = block_row[...]
     recv_sig[me] = thirds[me]
+
+    def rows_copy(k):
+        peer = (me + k) % N
+        return pltpu.make_async_remote_copy(
+            src_ref=sent_rows.at[peer],
+            dst_ref=recv_rows.at[me],
+            send_sem=sig_send.at[2, peer],
+            recv_sem=sig_recv.at[2, me],
+            device_id={"seq": peer},
+        )
+
+    def rows_arrival(k):
+        peer = (me + k) % N
+        return pltpu.make_async_remote_copy(
+            src_ref=sent_rows.at[peer],
+            dst_ref=recv_rows.at[peer],
+            send_sem=sig_send.at[2, peer],
+            recv_sem=sig_recv.at[2, peer],
+            device_id={"seq": peer},
+        )
+
+    def halo_copy(step):
+        return pltpu.make_async_remote_copy(
+            src_ref=tail_rows,
+            dst_ref=halo,
+            send_sem=halo_send,
+            recv_sem=halo_recv,
+            device_id={"seq": (me + step) % N},
+        )
 
     @pl.when(shift != 0)
     def _():
@@ -242,7 +282,7 @@
     for k in range(1, chips):
         tap_copy(k).start()
     for k in FAR:
-        third_copy(2, k).start()
+        rows_copy(k).start()
 
     def column_of(row):
         return jnp.sum(jnp.where(lanes16 == rows16 + me * N, row, 0.0), axis=1, keepdims=True)[None]
@@ -314,10 +354,6 @@
     passed[...] = scaled(gain[1], first)
     spec[1] = spectrum(1)
     ahead = filtered(forward(first), 1)
-    for k in FAR[::-1]:
-        third_arrival(2, k).wait_recv()
-    gate[...] = short(2)
-
     def out_copy(k):
         peer = (me + k) % N
         return pltpu.make_async_remote_copy(
@@ -338,24 +374,58 @@
             device_id={"seq": peer},
         )
 
-    gated[...] = (gate[...] * (dot(inv_a[...], ahead) + passed[...])).astype(BF16).reshape(N, N, W)
+    gated[...] = (dot(inv_a[...], ahead) + passed[...]).astype(BF16).reshape(N, N, W)
     for k in FAR:
         out_copy(k).start()
     own = pltpu.make_async_copy(gated.at[me], out.at[me], keep_sem)
     own.start()
 
+    up = lax.broadcasted_iota(jnp.int32, (W, W), 0)
+    place = (ids_row[...].reshape(W, W).astype(F32) == me.astype(F32)) & (up % N == sub % N)
+    for k in FAR[::-1]:
+        rows_arrival(k).wait_recv()
+    stream = dot(jnp.where(place, 1.0, 0.0).astype(BF16), recv_rows[...].reshape(W, W), ((0,), (0,)))
+    tail_rows[...] = stream[W - N :].astype(BF16)
+
+    @pl.when(me < N - 1)
+    def _():
+        halo_copy(1).start()
+
+    @pl.when(me == 0)
+    def _():
+        halo[...] = jnp.zeros_like(halo)
+
+    @pl.when(me > 0)
+    def _():
+        halo_copy(N - 1).wait_recv()
+
+    edge = halo[...].astype(F32)
+    one = jnp.where(up == 0, edge[N - 1 :], pltpu.roll(stream, 1, 0))
+    two = jnp.where(up == 0, edge[N - 2 : N - 1], jnp.where(up == 1, edge[N - 1 :], pltpu.roll(stream, 2, 0)))
+    tap = [short_filter[i : i + 1, 2 * W :] for i in range(3)]
+    gate[...] = (tap[0] * stream + tap[1] * one + tap[2] * two).T
+    aside = pltpu.make_async_copy(gate, side, side_sem)
+    aside.start()
+
     @pl.when(shift != 0)
     def _():
         tap_first().wait_send()
 
     each(N, lambda k: block_copy(k).wait_send())
-    for part in range(3):
+    for part in range(2):
         each(N, lambda k: third_copy(part, k).wait_send())
+    each(N, lambda k: rows_copy(k).wait_send())
+
+    @pl.when(me < N - 1)
+    def _():
+        halo_copy(1).wait_send()
+
     each(chips, lambda k: tap_copy(k).wait_send())
     each(N, lambda k: out_copy(k).wait_send())
     for k in FAR[::-1]:
         out_arrival(k).wait_recv()
     own.wait()
+    aside.wait()
 
 
 def body(n_batch, events, positions, length, filters, skip_gain, short_filter, in_proj, out_proj):
@@ -372,21 +442,25 @@
     ]
     dma = lambda *shape: pltpu.SemaphoreType.DMA(shape)
     held = [pltpu.VMEM((W, 2, 128) if i == 3 else x.shape, x.dtype) for i, x in enumerate(inputs)]
-    gated = pl.pallas_call(
+    second, gate = pl.pallas_call(
         functools.partial(kernel, n_batch),
-        out_shape=jax.ShapeDtypeStruct((N, N, W), BF16),
+        out_shape=(jax.ShapeDtypeStruct((N, N, W), BF16), jax.ShapeDtypeStruct((W, W), F32)),
         in_specs=[pl.BlockSpec(memory_space=pl.ANY)] * INPUTS,
-        out_specs=pl.BlockSpec(memory_space=pl.ANY),
+        out_specs=(pl.BlockSpec(memory_space=pl.ANY),) * 2,
         scratch_shapes=held
         + [
-            pltpu.VMEM((N, 3, N, W), BF16),
+            pltpu.VMEM((N, 2, N, W), BF16),
             pltpu.VMEM((1, W), jnp.int32),
             pltpu.VMEM((2, N, W), BF16),
             pltpu.VMEM((N, N, W), BF16),
             pltpu.VMEM((W, W), F32),
             pltpu.VMEM((W, W), F32),
             pltpu.VMEM((N, N, W), BF16),
-            pltpu.VMEM((N, 3, N, W), BF16),
+            pltpu.VMEM((N, N, W), BF16),
+            pltpu.VMEM((N, N, W), BF16),
+            pltpu.VMEM((N, W), BF16),
+            pltpu.VMEM((N, W), BF16),
+            pltpu.VMEM((N, 2, N, W), BF16),
             pltpu.VMEM((N, 1, W), jnp.int32),
             pltpu.VMEM((N, 2, N, W), BF16),
             pltpu.VMEM((2, W, 2 * W), F32),
@@ -400,6 +474,9 @@
             pltpu.SemaphoreType.DMA,
             pltpu.SemaphoreType.DMA,
             pltpu.SemaphoreType.DMA,
+            pltpu.SemaphoreType.DMA,
+            pltpu.SemaphoreType.DMA,
+            pltpu.SemaphoreType.DMA,
             dma(N),
             dma(N),
         ],
@@ -407,7 +484,8 @@
             collective_id=0, has_side_effects=True, vmem_limit_bytes=63 * 1024 * 1024
         ),
     )(*inputs)
-    return dot(gated.reshape(W, W), out_proj, ((0,), (0,))).astype(BF16)
+    gated = (gate * second.reshape(W, W).astype(F32)).astype(BF16)
+    return dot(gated, out_proj, ((0,), (0,))).astype(BF16)
 
 
 def solution(mesh):

time: 49.3 us -> 48.5 us (0.984)
  the two profiles are of different devices: /device:TPU:30 before, /device:TPU:14 now
where the time goes in v7:
time: 48.5 us; the launch traced here: 48.4 us
  Pallas kernels  45.8 us (94%)
  matrix products  1.87 us (4%)
  between operations  0.7 us (1%)
    pallas_call x1, Pallas kernels, body(): pl.pallas_call(functools.partial(kernel, n_batch), out_shape=(jax.ShapeDt...  45.8 us
    dot_general x1, matrix products, dot(): return lax.dot_general(a, b, (dims, ((), ())), preferred_element_type=F32)  1.87 us

profile of v7, /device:TPU:14, one launch (start us, length us, event | category | flops | bytes accessed | tf_op | source)
XLA Modules:
  0.0 48.4 jit_solution(8145332725815388302)
XLA Ops:
  0.0 0.0 copy-start
  0.7 45.8 %shard_map.127 = (bf16[16,16,256]{2,1,0:T(8,128)(2,1)}, f32[256,256]{1,0:T(8,128)}) custom-call(s32[1,1]{1,0:T(1,128)} %bitcast.5.refs_0_, s32[1,256]{1,0:T(1,128)} %bitcast.7, bf16[256,256]{1,0:T(8,128)(2,1)} %refs_2_.1, f32[256,2,256]{2,1,0:T(2,128)} %refs_3_.1, f32[2,256]{1,0:T(2,128)} %refs_4_.1, f32[3,768]{1,0:T(4,128)} %refs_5_.1, ...), custom_call_target="tpu_custom_call" | custom-call | tf_op jit(solution)/shard_map/pallas_call | solution.py:445
  46.5 0.0 copy-done
  46.5 1.9 %convolution_convert_fusion = bf16[256,256]{1,0:T(8,128)(2,1)} fusion(bf16[256,256]{1,0:T(8,128)(2,1)S(1)} %copy-done, f32[256,256]{1,0:T(8,128)} %get-tuple-element.7, bf16[256,256]{1,0:T(8,128)(2,1)} %bitcast.6), kind=kOutput, calls=%fused_computation | convolution fusion | flops 33816576 | bytes 655360 | tf_op jit(solution)/shard_map/dot_general | solution.py:55
Async XLA Ops:
  0.0 46.5 %copy-start = (bf16[256,256]{1,0:T(8,128)(2,1)S(1)}, bf16[256,256]{1,0:T(8,128)(2,1)}, u32[]{:S(2)}) copy-start(bf16[256,256]{1,0:T(8,128)(2,1)} %param.20) | copy-start | bytes 393220

commit v8 on v7

--- a/solution.py
+++ b/solution.py
@@ -98,12 +98,29 @@
     lane = lax.axis_index("batch")
     column, core = lane // 2, lane % 2
     chips = n_batch // 2
+    side_len = math.isqrt(chips)
+    plane = [(dy, dx) for dy in range(side_len) for dx in range(side_len) if dy or dx]
     shift = (column + N // 2 * core) % N
     target = (me + shift) % N
 
     barrier = pltpu.get_barrier_semaphore()
-    for k in FAR:
-        pl.semaphore_signal(barrier, inc=1, device_id={"seq": (me + k) % N})
+
+    def chip_at(dy, dx):
+        return (column // side_len + dy) % side_len * side_len + (column + dx) % side_len
+
+    hops = [(min(k, N - k), k) for k in FAR]
+    hops += [(min(dy, side_len - dy) + min(dx, side_len - dx), (dy, dx)) for dy, dx in plane]
+    hops.sort(key=lambda item: -item[0])
+
+    def greet(some):
+        for _, to in some:
+            if isinstance(to, tuple):
+                peer = {"batch": chip_at(*to) * 2 + core}
+            else:
+                peer = {"seq": (me + to) % N}
+            pl.semaphore_signal(barrier, inc=1, device_id=peer)
+
+    greet(hops[: len(hops) // 2])
     loads = []
     for i, (src, dst) in enumerate(zip(outside, inside)):
         if i == 3:
@@ -111,8 +128,7 @@
         loads.append(pltpu.make_async_copy(src, dst, load_sem.at[i]))
     for i in (1, 2, 6, 0, 3):
         loads[i].start()
-    for k in range(1, chips):
-        pl.semaphore_signal(barrier, inc=1, device_id={"batch": (lane + 2 * k) % n_batch})
+    greet(hops[len(hops) // 2 :])
     for i in (7, 11, 8, 5, 4, 9, 10):
         loads[i].start()
 
@@ -258,8 +274,7 @@
             device_id={"seq": target},
         ).wait_recv()
 
-    def tap_copy(k):
-        peer = (column + k) % chips
+    def tap_copy(peer):
         return pltpu.make_async_remote_copy(
             src_ref=recv_tap.at[slot],
             dst_ref=recv_tap.at[slot],
@@ -279,8 +294,9 @@
             device_id={"batch": peer * 2 + core},
         )
 
-    for k in range(1, chips):
-        tap_copy(k).start()
+    for _, to in hops:
+        if isinstance(to, tuple):
+            tap_copy(chip_at(*to)).start()
     for k in FAR:
         rows_copy(k).start()
 
@@ -420,7 +436,7 @@
     def _():
         halo_copy(1).wait_send()
 
-    each(chips, lambda k: tap_copy(k).wait_send())
+    each(chips, lambda k: tap_copy((column + k) % chips).wait_send())
     each(N, lambda k: out_copy(k).wait_send())
     for k in FAR[::-1]:
         out_arrival(k).wait_recv()

time: 48.5 us -> 48.6 us (level)
  the two profiles are of different devices: /device:TPU:14 before, /device:TPU:18 now
where the time goes in v8:
time: 48.6 us; the launch traced here: 48.5 us
  Pallas kernels  45.9 us (94%)
  matrix products  1.87 us (4%)
  between operations  0.7 us (1%)
    pallas_call x1, Pallas kernels, body(): pl.pallas_call(functools.partial(kernel, n_batch), out_shape=(jax.ShapeDt...  45.9 us
    dot_general x1, matrix products, dot(): return lax.dot_general(a, b, (dims, ((), ())), preferred_element_type=F32)  1.87 us

profile of v8, /device:TPU:18, one launch (start us, length us, event | category | flops | bytes accessed | tf_op | source)
XLA Modules:
  0.0 48.5 jit_solution(13144062573174327032)
XLA Ops:
  0.0 0.0 copy-start
  0.7 45.9 %shard_map.127 = (bf16[16,16,256]{2,1,0:T(8,128)(2,1)}, f32[256,256]{1,0:T(8,128)}) custom-call(s32[1,1]{1,0:T(1,128)} %bitcast.5.refs_0_, s32[1,256]{1,0:T(1,128)} %bitcast.7, bf16[256,256]{1,0:T(8,128)(2,1)} %refs_2_.1, f32[256,2,256]{2,1,0:T(2,128)} %refs_3_.1, f32[2,256]{1,0:T(2,128)} %refs_4_.1, f32[3,768]{1,0:T(4,128)} %refs_5_.1, ...), custom_call_target="tpu_custom_call" | custom-call | tf_op jit(solution)/shard_map/pallas_call | solution.py:461
  46.6 0.0 copy-done
  46.6 1.9 %convolution_convert_fusion = bf16[256,256]{1,0:T(8,128)(2,1)} fusion(bf16[256,256]{1,0:T(8,128)(2,1)S(1)} %copy-done, f32[256,256]{1,0:T(8,128)} %get-tuple-element.7, bf16[256,256]{1,0:T(8,128)(2,1)} %bitcast.6), kind=kOutput, calls=%fused_computation | convolution fusion | flops 33816576 | bytes 655360 | tf_op jit(solution)/shard_map/dot_general | solution.py:55
Async XLA Ops:
  0.0 46.6 %copy-start = (bf16[256,256]{1,0:T(8,128)(2,1)S(1)}, bf16[256,256]{1,0:T(8,128)(2,1)}, u32[]{:S(2)}) copy-start(bf16[256,256]{1,0:T(8,128)(2,1)} %param.20) | copy-start | bytes 393220

commit v9 on v8

--- a/solution.py
+++ b/solution.py
@@ -264,6 +264,9 @@
             device_id={"seq": (me + step) % N},
         )
 
+    for k in FAR:
+        rows_copy(k).start()
+
     @pl.when(shift != 0)
     def _():
         pltpu.make_async_remote_copy(
@@ -297,8 +300,6 @@
     for _, to in hops:
         if isinstance(to, tuple):
             tap_copy(chip_at(*to)).start()
-    for k in FAR:
-        rows_copy(k).start()
 
     def column_of(row):
         return jnp.sum(jnp.where(lanes16 == rows16 + me * N, row, 0.0), axis=1, keepdims=True)[None]
@@ -407,6 +408,16 @@
     def _():
         halo_copy(1).start()
 
+    tap = [short_filter[i : i + 1, 2 * W :] for i in range(3)]
+    one = jnp.where(up == 0, 0.0, pltpu.roll(stream, 1, 0))
+    two = jnp.where(up <= 1, 0.0, pltpu.roll(stream, 2, 0))
+    gate[...] = (tap[0] * stream + tap[1] * one + tap[2] * two).T
+    halves = [
+        pltpu.make_async_copy(gate.at[:, pl.ds(i * 128, 128)], side.at[:, pl.ds(i * 128, 128)], side_sem.at[i])
+        for i in range(2)
+    ]
+    halves[1].start()
+
     @pl.when(me == 0)
     def _():
         halo[...] = jnp.zeros_like(halo)
@@ -416,12 +427,10 @@
         halo_copy(N - 1).wait_recv()
 
     edge = halo[...].astype(F32)
-    one = jnp.where(up == 0, edge[N - 1 :], pltpu.roll(stream, 1, 0))
-    two = jnp.where(up == 0, edge[N - 2 : N - 1], jnp.where(up == 1, edge[N - 1 :], pltpu.roll(stream, 2, 0)))
-    tap = [short_filter[i : i + 1, 2 * W :] for i in range(3)]
-    gate[...] = (tap[0] * stream + tap[1] * one + tap[2] * two).T
-    aside = pltpu.make_async_copy(gate, side, side_sem)
-    aside.start()
+    last, ahead_of = edge[N - 1 :], edge[N - 2 : N - 1]
+    first_rows = jnp.where(up == 0, tap[1] * last + tap[2] * ahead_of, jnp.where(up == 1, tap[2] * last, 0.0))[:128]
+    gate[:, :128] += first_rows.T
+    halves[0].start()
 
     @pl.when(shift != 0)
     def _():
@@ -441,7 +450,8 @@
     for k in FAR[::-1]:
         out_arrival(k).wait_recv()
     own.wait()
-    aside.wait()
+    for half in halves:
+        half.wait()
 
 
 def body(n_batch, events, positions, length, filters, skip_gain, short_filter, in_proj, out_proj):
@@ -490,7 +500,7 @@
             pltpu.SemaphoreType.DMA,
             pltpu.SemaphoreType.DMA,
             pltpu.SemaphoreType.DMA,
-            pltpu.SemaphoreType.DMA,
+            dma(2),
             pltpu.SemaphoreType.DMA,
             pltpu.SemaphoreType.DMA,
             dma(N),

time: 48.6 us -> 48.7 us (level)
  no operation moved by 1% of the time
where the time goes in v9:
time: 48.7 us; the launch traced here: 48.5 us
  Pallas kernels  45.9 us (94%)
  matrix products  1.87 us (4%)
  between operations  0.7 us (1%)
    pallas_call x1, Pallas kernels, body(): pl.pallas_call(functools.partial(kernel, n_batch), out_shape=(jax.ShapeDt...  45.9 us
    dot_general x1, matrix products, dot(): return lax.dot_general(a, b, (dims, ((), ())), preferred_element_type=F32)  1.87 us

profile of v9, /device:TPU:18, one launch (start us, length us, event | category | flops | bytes accessed | tf_op | source)
XLA Modules:
  0.0 48.5 jit_solution(16909368347108930585)
XLA Ops:
  0.0 0.0 copy-start
  0.7 45.9 %shard_map.127 = (bf16[16,16,256]{2,1,0:T(8,128)(2,1)}, f32[256,256]{1,0:T(8,128)}) custom-call(s32[1,1]{1,0:T(1,128)} %bitcast.5.refs_0_, s32[1,256]{1,0:T(1,128)} %bitcast.7, bf16[256,256]{1,0:T(8,128)(2,1)} %refs_2_.1, f32[256,2,256]{2,1,0:T(2,128)} %refs_3_.1, f32[2,256]{1,0:T(2,128)} %refs_4_.1, f32[3,768]{1,0:T(4,128)} %refs_5_.1, ...), custom_call_target="tpu_custom_call" | custom-call | tf_op jit(solution)/shard_map/pallas_call | solution.py:471
  46.6 0.0 copy-done
  46.6 1.9 %convolution_convert_fusion = bf16[256,256]{1,0:T(8,128)(2,1)} fusion(bf16[256,256]{1,0:T(8,128)(2,1)S(1)} %copy-done, f32[256,256]{1,0:T(8,128)} %get-tuple-element.7, bf16[256,256]{1,0:T(8,128)(2,1)} %bitcast.6), kind=kOutput, calls=%fused_computation | convolution fusion | flops 33816576 | bytes 655360 | tf_op jit(solution)/shard_map/dot_general | solution.py:55
Async XLA Ops:
  0.0 46.6 %copy-start = (bf16[256,256]{1,0:T(8,128)(2,1)S(1)}, bf16[256,256]{1,0:T(8,128)(2,1)}, u32[]{:S(2)}) copy-start(bf16[256,256]{1,0:T(8,128)(2,1)} %param.20) | copy-start | bytes 393220

commit v10 on v9

--- a/solution.py
+++ b/solution.py
@@ -264,9 +264,6 @@
             device_id={"seq": (me + step) % N},
         )
 
-    for k in FAR:
-        rows_copy(k).start()
-
     @pl.when(shift != 0)
     def _():
         pltpu.make_async_remote_copy(
@@ -300,6 +297,8 @@
     for _, to in hops:
         if isinstance(to, tuple):
             tap_copy(chip_at(*to)).start()
+    for k in FAR:
+        rows_copy(k).start()
 
     def column_of(row):
         return jnp.sum(jnp.where(lanes16 == rows16 + me * N, row, 0.0), axis=1, keepdims=True)[None]
@@ -315,12 +314,16 @@
         return dot(jnp.concatenate([x, x], axis=1), table[...])
 
     def forward(signal):
-        if signal.dtype == BF16:
-            mid = dot(fwd_a[:, W:], jnp.concatenate([signal, signal], axis=0))
-        else:
-            mid = dot(fwd_a[...], parts(signal, 0))
-        re, im = rotate(mid[:W], mid[W:], 1.0)
-        return inner(re, im, fwd_b)
+        mid = dot(fwd_a[...], parts(signal, 0))
+        return inner(*rotate(mid[:W], mid[W:], 1.0), fwd_b)
+
+    def spectra():
+        sides = []
+        for f in range(2):
+            lags = recv_tap[:, f].reshape(W, W)
+            mid = dot(fwd_a[:, W:], jnp.concatenate([lags, lags], axis=0))
+            sides.append(rotate(mid[:W], mid[W:], 1.0))
+        spec[...] = inner(*(jnp.concatenate(x, axis=0) for x in zip(*sides)), fwd_b).reshape(2, W, 2 * W)
 
     def filtered(got, f):
         re, im = got[:, :W], got[:, W:]
@@ -351,7 +354,6 @@
         loads[i].wait()
     gain = [column_of(skip_gain[i : i + 1, :]) for i in range(2)]
     scaled = lambda g, x: (g * x.reshape(-1, N, W)).reshape(-1, W)
-    spectrum = lambda f: forward(recv_tap[:, f].reshape(W, W))
 
     for k in FAR[::-1]:
         block_arrival(k).wait_recv()
@@ -366,10 +368,9 @@
     gate[...] = short(1)
     for k in range(1, chips):
         tap_arrival(k).wait_recv()
-    spec[0] = spectrum(0)
+    spectra()
     first = gate[...] * (dot(inv_a[...], filtered(ahead, 0)) + scaled(gain[0], value))
     passed[...] = scaled(gain[1], first)
-    spec[1] = spectrum(1)
     ahead = filtered(forward(first), 1)
     def out_copy(k):
         peer = (me + k) % N

time: 48.7 us -> 48.6 us (level)
  the two profiles are of different devices: /device:TPU:18 before, /device:TPU:14 now
where the time goes in v10:
time: 48.6 us; the launch traced here: 48.3 us
  Pallas kernels  45.8 us (94%)
  matrix products  1.87 us (4%)
  between operations  0.7 us (1%)
    pallas_call x1, Pallas kernels, body(): pl.pallas_call(functools.partial(kernel, n_batch), out_shape=(jax.ShapeDt...  45.8 us
    dot_general x1, matrix products, dot(): return lax.dot_general(a, b, (dims, ((), ())), preferred_element_type=F32)  1.87 us

profile of v10, /device:TPU:14, one launch (start us, length us, event | category | flops | bytes accessed | tf_op | source)
XLA Modules:
  0.0 48.3 jit_solution(9409242713794914331)
XLA Ops:
  0.0 0.0 copy-start
  0.7 45.8 %shard_map.127 = (bf16[16,16,256]{2,1,0:T(8,128)(2,1)}, f32[256,256]{1,0:T(8,128)}) custom-call(s32[1,1]{1,0:T(1,128)} %bitcast.5.refs_0_, s32[1,256]{1,0:T(1,128)} %bitcast.7, bf16[256,256]{1,0:T(8,128)(2,1)} %refs_2_.1, f32[256,2,256]{2,1,0:T(2,128)} %refs_3_.1, f32[2,256]{1,0:T(2,128)} %refs_4_.1, f32[3,768]{1,0:T(4,128)} %refs_5_.1, ...), custom_call_target="tpu_custom_call" | custom-call | tf_op jit(solution)/shard_map/pallas_call | solution.py:472
  46.5 0.0 copy-done
  46.5 1.9 %convolution_convert_fusion = bf16[256,256]{1,0:T(8,128)(2,1)} fusion(bf16[256,256]{1,0:T(8,128)(2,1)S(1)} %copy-done, f32[256,256]{1,0:T(8,128)} %get-tuple-element.7, bf16[256,256]{1,0:T(8,128)(2,1)} %bitcast.6), kind=kOutput, calls=%fused_computation | convolution fusion | flops 33816576 | bytes 655360 | tf_op jit(solution)/shard_map/dot_general | solution.py:55
Async XLA Ops:
  0.0 46.5 %copy-start = (bf16[256,256]{1,0:T(8,128)(2,1)S(1)}, bf16[256,256]{1,0:T(8,128)(2,1)}, u32[]{:S(2)}) copy-start(bf16[256,256]{1,0:T(8,128)(2,1)} %param.20) | copy-start | bytes 393220
